TPU v7x, 256 devices: a whole 4x4x8 slice. The times are simulated.
256 devices in a mesh: section: 16 (over z, core), tensor: 8 (over y, x_lo), dp: 2 (over x_hi).
Axes of the slice: x: 4 (x_hi: 2, x_lo: 2; x = x_hi * 2 + x_lo), y: 4, z: 8, core: 2. Of those that a mesh axis runs over, the one named last changes fastest.
Arguments:
- old_master: float32 [12288, 8192], P('section', ('tensor', 'dp')), may hold values from -0.0546875 to 0.0546875
- old_first: float32 [12288, 8192], P('section', ('tensor', 'dp')), may hold values from -0.3 to 0.3
- old_second: float32 [12288, 8192], P('section', ('tensor', 'dp')), may hold values from 0.001 to 0.01
- dest_section: int32 [96], replicated, may hold values from 0 to 15, as said below
- dest_offset: int32 [96], replicated, may hold values from 0 to 7, as said below
- hidden_acts: bfloat16 [2, 1024, 16384], P('dp', None, 'section'), may hold values from -6 to 6
- out_grad: bfloat16 [2, 1024, 8192], P('dp', None, 'tensor'), may hold values from -6 to 6
Outputs:
- proj_out: bfloat16 [2, 1024, 8192], P('dp', 'section', 'tensor')
- hidden_grad: bfloat16 [2, 1024, 16384], P('dp', None, ('section', 'tensor'))
- adam_step: float32 [16384, 8192], P('section', ('tensor', 'dp'))
Inputs may be any that keep to these rules, and one draw needn't show every extreme that they name: `dest_section`: no new owner receives more than 8 blocks and some receive exactly 8; one old owner sends at most 1 block to any one new owner; every new owner receives some block. `dest_offset`: the blocks that go to one new owner have distinct slots.
All inputs are finite; a program needn't handle non-finite values.
Results may differ from a plain program's by a relative error of at most 0.0049.
Values may be sent and summed in bfloat16 or wider, within the bound.
A program may use at most 128 MiB of HBM per device.

v0:
```python
import jax
import jax.numpy as jnp
from jax import lax
from jax.sharding import PartitionSpec as P

ROWS = 128
BLOCKS = 6
CAP = 1
RCAP = 8


CORR_FIRST = 1.0
CORR_SECOND = 0.6323045752


def shards(old_master, old_first, old_second, dest_section, dest_offset, hidden_acts, out_grad):
    sections = lax.axis_size("section")
    section_here = lax.axis_index("section")
    width = old_master.shape[1]
    slots = sections * CAP
    targets = dest_section.reshape(sections, BLOCKS)
    earlier = jnp.arange(BLOCKS)[None, :] < jnp.arange(BLOCKS)[:, None]
    same_dest = targets[:, :, None] == targets[:, None, :]
    ranks = jnp.sum(same_dest & earlier[None], axis=2)
    own_dest = lax.dynamic_index_in_dim(targets, section_here, 0, keepdims=False)
    own_rank = lax.dynamic_index_in_dim(ranks, section_here, 0, keepdims=False)
    packing = (jnp.arange(slots)[:, None] == (own_dest * CAP + own_rank)[None, :]).astype(
        jnp.float32
    )

    def packed(state):
        return jnp.dot(
            packing, state.reshape(BLOCKS, ROWS * width), precision=lax.Precision.HIGHEST
        )

    source_slot = (jnp.arange(sections)[:, None] * CAP + ranks).reshape(-1)
    arriving = (targets == section_here).reshape(-1)
    to_slot = (jnp.arange(RCAP)[:, None] == dest_offset[None, :]) & arriving[None, :]
    from_slot = source_slot[:, None] == jnp.arange(slots)[None, :]
    placing = jnp.dot(to_slot.astype(jnp.float32), from_slot.astype(jnp.float32))
    used_rows = jnp.repeat(jnp.sum(to_slot.astype(jnp.float32), axis=1), ROWS)[:, None]

    def placed(received):
        return jnp.dot(placing, received, precision=lax.Precision.HIGHEST).reshape(
            RCAP * ROWS, width
        )

    moved = (
        lax.all_to_all(packed(old_master), "section", split_axis=0, concat_axis=0, tiled=True),
        lax.all_to_all(packed(old_first), "section", split_axis=0, concat_axis=0, tiled=True),
        lax.all_to_all(packed(old_second), "section", split_axis=0, concat_axis=0, tiled=True),
    )
    master_new = placed(moved[0])
    weight = master_new.astype(jnp.bfloat16)
    acts_in = hidden_acts[0]
    grad_in = out_grad[0]
    tokens_here = acts_in.shape[0]
    replicas = lax.axis_size("dp")
    full_weight = lax.all_gather(weight, "dp", axis=1, tiled=True)
    proj_out = lax.psum_scatter(
        jnp.dot(acts_in, full_weight, preferred_element_type=jnp.float32),
        "section",
        scatter_dimension=0,
        tiled=True,
    ).astype(jnp.bfloat16)[None]
    partial_value = jnp.einsum(
        "tc,kc->tk", grad_in, full_weight, preferred_element_type=jnp.float32
    )
    hidden_grad = lax.psum_scatter(partial_value, "tensor", scatter_dimension=1, tiled=True).astype(
        jnp.bfloat16
    )
    term = jnp.einsum("tk,tc->kc", acts_in, grad_in, preferred_element_type=jnp.float32) / float(
        replicas * tokens_here
    )
    grad = lax.psum_scatter(
        term.astype(jnp.bfloat16), "dp", scatter_dimension=1, tiled=True
    ).astype(jnp.float32)
    first_new = placed(moved[1])
    second_new = placed(moved[2])
    first = 0.9 * first_new + 0.1 * grad
    second = 0.999 * second_new + 0.001 * grad * grad
    adam_step = used_rows * (first / CORR_FIRST) / (jnp.sqrt(second / CORR_SECOND) + 1e-08)
    return (proj_out, hidden_grad[None], adam_step)


def solution(mesh):
    placed = (
        P("section", ("tensor", "dp")),
        P("section", ("tensor", "dp")),
        P("section", ("tensor", "dp")),
        P(),
        P(),
        P("dp", None, "section"),
        P("dp", None, "tensor"),
    )
    return jax.shard_map(
        shards,
        mesh=mesh,
        in_specs=placed,
        out_specs=(
            P("dp", "section", "tensor"),
            P("dp", None, ("section", "tensor")),
            P("section", ("tensor", "dp")),
        ),
        check_vma=False,
    )
```

profile of v0, /device:TPU:1, one launch (start us, length us, event | category | flops | bytes accessed | tf_op | source)
XLA Modules:
  0.0 473.5 jit_solution(14432730846429837593)
XLA Ops:
  7.2 0.0 copy-start
  7.2 0.9 eq.67
  8.1 0.1 copy.28
  8.2 3.5 reshape.61
  11.7 0.1 convert_reduce_fusion
  11.8 0.2 add_reduce_fusion
  12.0 3.4 convolution_bitcast_fusion.2
  15.4 6.3 %copy.32 = f32[16,1,65536]{2,1,0:T(1,128)} copy(f32[16,1,65536]{2,0,1:T(8,128)S(1)} %convolution_bitcast_fusion.2) | data formatting | bytes 8388608 | tf_op jit(solution)/shard_map/all_to_all | solution.py:49
  21.7 0.0 copy-start.2
  21.7 0.0 copy-start.4
  21.7 10.1 %all-to-all-start = ((f32[16,1,65536]{2,1,0:T(1,128)}), f32[16,1,65536]{2,1,0:T(1,128)}, u32[]{:S(2)}, u32[]{:S(2)}) async-start(f32[16,1,65536]{2,1,0:T(1,128)} %copy.32), calls=%async_computation | async-start | bytes 8388608 | tf_op jit(solution)/shard_map/all_to_all | solution.py:49
  31.8 0.3 all-gather.2.cloned.1.call-start
  32.2 0.1 copy.30
  32.3 0.1 add.46
  32.4 0.0 copy-done.2
  32.4 0.0 copy-done.4
  32.4 0.2 fusion.17
  32.6 92.8 %all-to-all-done = f32[16,1,65536]{2,1,0:T(1,128)} async-done(((f32[16,1,65536]{2,1,0:T(1,128)}), f32[16,1,65536]{2,1,0:T(1,128)}, u32[]{:S(2)}, u32[]{:S(2)}) %all-to-all-start) | async-done | bytes 4194336 | tf_op jit(solution)/shard_map/all_to_all | solution.py:49
  125.4 6.4 %convolution_convert_fusion = bf16[8,65536]{1,0:T(8,128)(2,1)S(1)} fusion(f32[8,16]{1,0:T(8,128)S(1)} %fusion.17, f32[16,1,65536]{2,1,0:T(1,128)} %all-to-all-done), kind=kOutput, calls=%fused_computation.5 | convolution fusion | flops 101187584 | bytes 5243392 | tf_op jit(solution)/shard_map/dot_general | solution.py:44
  131.9 1.5 convert_element_type.29
  133.3 0.0 all-gather.2.cloned.1.call-update
  133.3 0.6 reduce-scatter.8.cloned.1.call-start
  133.9 0.0 copy-done
  133.9 5.3 %multiply_convert_fusion = bf16[1024,1024]{1,0:T(8,128)(2,1)} fusion(bf16[1,1024,1024]{2,1,0:T(8,128)(2,1)} %param.13, bf16[1,1024,1024]{2,1,0:T(8,128)(2,1)S(1)} %copy-done), kind=kOutput, calls=%fused_computation.12 | convolution fusion | flops 2149580800 | bytes 6291456 | tf_op jit(solution)/shard_map/tk,tc->kc/dot_general | solution.py:72
  139.2 0.0 reduce-scatter.8.cloned.1.call-update
  139.3 3.5 reshape.62
  142.8 3.5 convolution_bitcast_fusion.1
  146.3 6.3 %copy.33 = f32[16,1,65536]{2,1,0:T(1,128)} copy(f32[16,1,65536]{2,0,1:T(8,128)S(1)} %convolution_bitcast_fusion.1) | data formatting | bytes 8388608 | tf_op jit(solution)/shard_map/all_to_all | solution.py:50
  152.6 5.5 %all-to-all-start.1 = ((f32[16,1,65536]{2,1,0:T(1,128)}), f32[16,1,65536]{2,1,0:T(1,128)}, u32[]{:S(2)}, u32[]{:S(2)}) async-start(f32[16,1,65536]{2,1,0:T(1,128)} %copy.33), calls=%async_computation.2 | async-start | bytes 8388608 | tf_op jit(solution)/shard_map/all_to_all | solution.py:50
  158.0 0.2 reduce-scatter.10.cloned.1.call-start
  158.3 14.3 %all-gather.2.cloned.1.call-done = bf16[1024,1024]{1,0:T(8,128)(2,1)} async-done(((bf16[1024,512]{1,0:T(8,128)(2,1)}), bf16[1024,1024]{1,0:T(8,128)(2,1)}) %all-gather.2.cloned.1.call-update) | async-done | bytes 2097168 | tf_op jit(solution)/shard_map/all_gather | solution.py:59
  172.6 5.9 %convolution_bitcast_fusion.4 = f32[1024,1024]{0,1:T(8,128)} fusion(bf16[1024,1024]{1,0:T(8,128)(2,1)} %all-gather.2.cloned.1.call-done, bf16[1,1024,1024]{2,1,0:T(8,128)(2,1)S(1)} %copy-done), kind=kOutput, calls=%fused_computation.16 | convolution fusion | flops 2147483648 | bytes 8388608 | tf_op jit(solution)/shard_map/dot_general | solution.py:61
  178.5 5.3 %copy.37 = f32[1024,1024]{1,0:T(8,128)} copy(f32[1024,1024]{0,1:T(8,128)} %convolution_bitcast_fusion.4) | data formatting | bytes 8388608
  183.8 0.0 reduce-scatter.10.cloned.1.call-update
  183.8 2.2 reshape.63
  186.1 1.8 convolution_bitcast_fusion
  187.9 6.3 %copy.34 = f32[16,1,65536]{2,1,0:T(1,128)} copy(f32[16,1,65536]{2,0,1:T(8,128)S(1)} %convolution_bitcast_fusion) | data formatting | bytes 8388608 | tf_op jit(solution)/shard_map/all_to_all | solution.py:51
  194.2 0.0 copy-start.3
  194.2 62.2 %all-to-all-done.1 = f32[16,1,65536]{2,1,0:T(1,128)} async-done(((f32[16,1,65536]{2,1,0:T(1,128)}), f32[16,1,65536]{2,1,0:T(1,128)}, u32[]{:S(2)}, u32[]{:S(2)}) %all-to-all-start.1) | async-done | bytes 4194336 | tf_op jit(solution)/shard_map/all_to_all | solution.py:50
  256.4 6.8 %all-to-all-start.2 = ((f32[16,1,65536]{2,1,0:T(1,128)}), f32[16,1,65536]{2,1,0:T(1,128)}, u32[]{:S(2)}, u32[]{:S(2)}) async-start(f32[16,1,65536]{2,1,0:T(1,128)} %copy.34), calls=%async_computation.4 | async-start | bytes 8388608 | tf_op jit(solution)/shard_map/all_to_all | solution.py:51
  263.1 0.2 reduce-scatter.6.cloned.1.call-start
  263.4 0.0 copy-done.3
  263.4 6.0 %convolution_bitcast_fusion.3 = f32[1024,1024]{0,1:T(8,128)} fusion(bf16[1024,1024]{1,0:T(8,128)(2,1)} %all-gather.2.cloned.1.call-done, bf16[1,1024,1024]{2,1,0:T(8,128)(2,1)S(1)} %copy-done.3), kind=kOutput, calls=%fused_computation.15 | convolution fusion | flops 2147483648 | bytes 8388608 | tf_op jit(solution)/shard_map/tc,kc->tk/dot_general | solution.py:66
  269.4 0.0 reduce-scatter.6.cloned.1.call-update
  269.4 0.1 convert_reduce_fusion.1
  269.5 0.1 broadcast_bitcast_fusion
  269.6 6.8 %convolution_multiply_fusion.1 = f32[8,65536]{1,0:T(8,128)S(1)} fusion(f32[8,16]{1,0:T(8,128)S(1)} %fusion.17, f32[16,1,65536]{2,1,0:T(1,128)} %all-to-all-done.1), kind=kOutput, calls=%fused_computation.4 | convolution fusion | flops 101187584 | bytes 6291968 | tf_op jit(solution)/shard_map/dot_general | solution.py:44
  276.4 1.7 mul.47
  278.1 91.5 %all-to-all-done.2 = f32[16,1,65536]{2,1,0:T(1,128)} async-done(((f32[16,1,65536]{2,1,0:T(1,128)}), f32[16,1,65536]{2,1,0:T(1,128)}, u32[]{:S(2)}, u32[]{:S(2)}) %all-to-all-start.2) | async-done | bytes 4194336 | tf_op jit(solution)/shard_map/all_to_all | solution.py:51
  369.6 6.8 %convolution_multiply_fusion = f32[8,65536]{1,0:T(8,128)S(1)} fusion(f32[8,16]{1,0:T(8,128)S(1)} %fusion.17, f32[16,1,65536]{2,1,0:T(1,128)} %all-to-all-done.2), kind=kOutput, calls=%fused_computation.3 | convolution fusion | flops 101187584 | bytes 6291968 | tf_op jit(solution)/shard_map/dot_general | solution.py:44
  376.4 1.7 mul.53
  378.1 0.0 reduce-scatter.8.cloned.1.call-done
  378.1 0.0 copy-start.1
  378.1 5.2 %fusion.8 = f32[1024,512]{1,0:T(8,128)} fusion(f32[1024,512]{1,0:T(8,128)} %mul.47, bf16[1024,512]{1,0:T(8,128)(2,1)} %reduce-scatter.8.cloned.1.call-done, f32[1024,512]{1,0:T(8,128)} %mul.53, f32[1024]{0:T(1024)S(1)} %broadcast_bitcast_fusion), kind=kLoop, calls=%fused_computation.19 | loop fusion | flops 5242880 | bytes 7344128 | tf_op jit(solution)/shard_map/div | solution.py:82
  383.4 0.0 reduce-scatter.10.cloned.1.call-done
  383.4 1.1 copy.38
  384.5 0.8 copy.35
  385.3 79.6 %reduce-scatter.6.cloned.1.call-done = f32[1024,128]{0,1:T(8,128)} async-done(((f32[1024,1024]{0,1:T(8,128)}), f32[1024,128]{0,1:T(8,128)}) %reduce-scatter.6.cloned.1.call-update) | async-done | bytes 524304 | tf_op jit(solution)/shard_map/reduce_scatter | solution.py:69
  464.9 1.1 convert_bitcast_fusion
  465.9 0.8 copy.36
  466.8 0.0 copy-done.1
  (3 shorter events, 0.0 us)
Async XLA Ops:
  7.2 126.8 %copy-start = (bf16[1,1024,1024]{2,1,0:T(8,128)(2,1)S(1)}, bf16[1,1024,1024]{2,1,0:T(8,128)(2,1)}, u32[]{:S(2)}) copy-start(bf16[1,1024,1024]{2,1,0:T(8,128)(2,1)} %param.12) | copy-start | bytes 6291460
  21.7 10.6 %copy-start.2 = (s32[96]{0:T(128)S(1)}, s32[96]{0:T(128)}, u32[]{:S(2)}) copy-start(s32[96]{0:T(128)} %param.10) | copy-start | bytes 1156
  21.7 10.7 %copy-start.4 = (s32[96]{0:T(128)S(1)}, s32[96]{0:T(128)}, u32[]{:S(2)}) copy-start(s32[96]{0:T(128)} %param.11) | copy-start | bytes 1156
  21.7 103.7 %all-to-all-start = ((f32[16,1,65536]{2,1,0:T(1,128)}), f32[16,1,65536]{2,1,0:T(1,128)}, u32[]{:S(2)}, u32[]{:S(2)}) async-start(f32[16,1,65536]{2,1,0:T(1,128)} %copy.32), calls=%async_computation | async-start | bytes 8388608 | tf_op jit(solution)/shard_map/all_to_all | solution.py:49
  31.8 140.7 %all-gather.2.cloned.1.call-start = ((), (), s32[]{:S(2)}) async-start(), calls=%async_computation.6 | async-start | bytes 3145728 | tf_op jit(solution)/shard_map/all_gather | solution.py:59
  133.3 244.8 %reduce-scatter.8.cloned.1.call-start = ((), (), s32[]{:S(2)}) async-start(), calls=%async_computation.8 | async-start | bytes 3145728 | tf_op jit(solution)/shard_map/reduce_scatter | solution.py:75
  152.6 103.8 %all-to-all-start.1 = ((f32[16,1,65536]{2,1,0:T(1,128)}), f32[16,1,65536]{2,1,0:T(1,128)}, u32[]{:S(2)}, u32[]{:S(2)}) async-start(f32[16,1,65536]{2,1,0:T(1,128)} %copy.33), calls=%async_computation.2 | async-start | bytes 8388608 | tf_op jit(solution)/shard_map/all_to_all | solution.py:50
  158.0 225.3 %reduce-scatter.10.cloned.1.call-start = ((), (), s32[]{:S(2)}) async-start(), calls=%async_computation.9 | async-start | bytes 4456448
  194.2 69.2 %copy-start.3 = (bf16[1,1024,1024]{2,1,0:T(8,128)(2,1)S(1)}, bf16[1,1024,1024]{2,1,0:T(8,128)(2,1)}, u32[]{:S(2)}) copy-start(bf16[1,1024,1024]{2,1,0:T(8,128)(2,1)} %param.13) | copy-start | bytes 6291460
  256.4 113.2 %all-to-all-start.2 = ((f32[16,1,65536]{2,1,0:T(1,128)}), f32[16,1,65536]{2,1,0:T(1,128)}, u32[]{:S(2)}, u32[]{:S(2)}) async-start(f32[16,1,65536]{2,1,0:T(1,128)} %copy.34), calls=%async_computation.4 | async-start | bytes 8388608 | tf_op jit(solution)/shard_map/all_to_all | solution.py:51
  263.1 201.7 %reduce-scatter.6.cloned.1.call-start = ((), (), s32[]{:S(2)}) async-start(), calls=%async_computation.7 | async-start | bytes 4718592 | tf_op jit(solution)/shard_map/reduce_scatter | solution.py:69
  378.1 88.6 %copy-start.1 = (bf16[1,1024,1024]{2,1,0:T(8,128)(2,1)S(1)}, bf16[1,1024,1024]{2,1,0:T(8,128)(2,1)}, u32[]{:S(2)}) copy-start(bf16[1,1024,1024]{2,1,0:T(8,128)(2,1)} %param.12) | copy-start | bytes 6291460
Sparse Core Ops, SparseCore 0:
  133.5 39.0 all-gather.1
  175.0 37.8 reduce-scatter.7
  215.7 152.2 reduce-scatter.9
  370.6 94.2 reduce-scatter.5
where the time goes:
time: 480 us; the launch traced here: 474 us
  waiting for transfers between devices  340 us (71%)
  matrix products  46.3 us (10%)
  local copies, waits for them, and re-layouts  42.3 us (9%)
  starting transfers between devices  23.7 us (5%)
  between operations  14.1 us (3%)
  other arithmetic  6.72 us (1%)
    all_to_all x1, waiting for transfers between devices, shards(): lax.all_to_all(packed(old_master), 'section', split_axis=0, concat_axis=0...  92.8 us
    all_to_all x1, waiting for transfers between devices, shards(): lax.all_to_all(packed(old_second), 'section', split_axis=0, concat_axis=0...  91.5 us
    reduce_scatter x1, waiting for transfers between devices, shards(): lax.psum_scatter(partial_value, 'tensor', scatter_dimension=1, tiled=True)  79.6 us
    all_to_all x1, waiting for transfers between devices, shards(): lax.all_to_all(packed(old_first), 'section', split_axis=0, concat_axis=0,...  62.2 us
    dot_general x3, matrix products, placed(): jnp.dot(placing, received, precision=lax.Precision.HIGHEST)  20.1 us
    all_gather x1, waiting for transfers between devices, shards(): full_weight = lax.all_gather(weight, 'dp', axis=1, tiled=True)  14.3 us
    all_to_all x1, starting transfers between devices, shards(): lax.all_to_all(packed(old_master), 'section', split_axis=0, concat_axis=0...  10.1 us
  transfers between devices with their start and end apart: 7, of which 5 were waited for; matrix products, arithmetic and copies ran while one was open for 15% of the time, Pallas kernels for 0%

commit v1 on v0

v1 whole, which is shorter than its diff:
```python
import jax
import jax.numpy as jnp
from jax import lax
from jax.experimental import pallas as pl
from jax.experimental.pallas import tpu as pltpu
from jax.sharding import PartitionSpec as P

ROWS = 128
BLOCKS = 6
RCAP = 8
CORR_SECOND = 0.6323045752
MESH = pl.DeviceIdType.MESH
BF = jnp.bfloat16
F32 = jnp.float32


def plan(dest_ref, off_ref, tab):
    s = lax.axis_index("section")
    for i in range(64):
        tab[i] = 0

    def owner(o, _):
        for b in range(BLOCKS):
            g = o * BLOCKS + b

            @pl.when(dest_ref[g] == s)
            def _():
                k = off_ref[g]
                tab[o] = k
                tab[32 + k] = o
                tab[40 + k] = 1

        return 0

    lax.fori_loop(0, 16, owner, 0)
    for b in range(BLOCKS):
        p = dest_ref[s * BLOCKS + b]
        tab[16 + p] = b
        tab[48 + b] = p


def kernel(
    tab, master, first, second, acts, grads,
    proj_out, hidden_out, step_out,
    strip, blk, mv, gv, fv, sv,
    send1, recv1, aold, wf, gsend, grecv, gown, pk, pown, cp, q, rq,
    hgs, hgr, hb, send3, recv3, send5, hgf, ab, send4, recv4,
    lsem, ss1, rs1, ss2, rs2, xss, xrs, ssq, rsq, ssh, rsh, ss3, rs3, ss5, rs5, ss4, rs4,
):
    ns, nt = 16, 8
    s = lax.axis_index("section")
    t = lax.axis_index("tensor")
    d = lax.axis_index("dp")
    z, c = s // 2, s % 2
    od = 1 - d
    core_peer = (z * 2 + (1 - c), t, d)
    dp_peer = (s, t, od)

    def sec(k):
        return lax.rem(s + k, ns)

    def ten(k):
        return lax.rem(t + k, nt)

    trow = pl.multiple_of(t * 128, 128)
    locals_ = [
        pltpu.make_async_copy(acts.at[pl.ds(trow, 128)], strip, lsem.at[0]),
        pltpu.make_async_copy(master, mv, lsem.at[1]),
        pltpu.make_async_copy(grads, gv, lsem.at[2]),
        pltpu.make_async_copy(first, fv, lsem.at[3]),
        pltpu.make_async_copy(second, sv, lsem.at[4]),
    ]
    for cpy in locals_:
        cpy.start()

    bar = pltpu.get_barrier_semaphore()
    for k in range(1, ns):
        pl.semaphore_signal(bar, inc=1, device_id=(sec(k), t, d), device_id_type=MESH)
    for k in range(1, nt):
        pl.semaphore_signal(bar, inc=1, device_id=(s, ten(k), d), device_id_type=MESH)
    pl.semaphore_signal(bar, inc=1, device_id=dp_peer, device_id_type=MESH)

    slot_of = [tab[o] for o in range(ns)]
    block_for = [tab[16 + p] for p in range(ns)]
    owner_of = [tab[32 + k] for k in range(RCAP)]
    used = [tab[40 + k].astype(F32) for k in range(RCAP)]
    mine = [tab[48 + b] for b in range(BLOCKS)]

    locals_[0].wait()
    for k in range(RCAP):
        blk[k] = strip[:, pl.ds(k * 128, 128)]
    for o in range(ns):
        send1[o] = blk[slot_of[o]]
    locals_[1].wait()
    for b in range(BLOCKS):
        wf[d, pl.ds(b * 128, 128)] = mv[pl.ds(b * 128, 128)].astype(BF)

    pl.semaphore_wait(bar, ns - 1 + nt - 1 + 1)

    def to_sections(src, dst, sends, recvs):
        def copy(p):
            return pltpu.make_async_remote_copy(
                src_ref=src.at[p], dst_ref=dst.at[s],
                send_sem=sends.at[p], recv_sem=recvs.at[s],
                device_id=(p, t, d), device_id_type=MESH)

        def go(k, _):
            copy(sec(k)).start()
            return 0

        def wait_send(k, _):
            copy(sec(k)).wait_send()
            return 0

        def wait_recv(k, _):
            p = sec(k)
            pltpu.make_async_remote_copy(
                src_ref=src.at[p], dst_ref=dst.at[p],
                send_sem=sends.at[p], recv_sem=recvs.at[p],
                device_id=(p, t, d), device_id_type=MESH).wait_recv()
            return 0

        return (
            lambda: lax.fori_loop(1, ns, go, 0),
            lambda: lax.fori_loop(1, ns, wait_send, 0),
            lambda: lax.fori_loop(1, ns, wait_recv, 0),
        )

    go1, ws1, wr1 = to_sections(send1, recv1, ss1, rs1)
    go1()
    wcopy = pltpu.make_async_remote_copy(
        src_ref=wf.at[d], dst_ref=wf.at[d], send_sem=xss.at[0], recv_sem=xrs.at[0],
        device_id=dp_peer, device_id_type=MESH)
    wcopy.start()
    recv1[s] = send1[s]
    wr1()
    for b in range(BLOCKS):
        aold[pl.ds(trow, 128), pl.ds(b * 128, 128)] = recv1[mine[b]]

    def gather(p, q_):
        row = pl.multiple_of(q_ * 128, 128)
        return pltpu.make_async_remote_copy(
            src_ref=aold.at[pl.ds(row, 128)], dst_ref=aold.at[pl.ds(row, 128)],
            send_sem=ss2.at[p], recv_sem=rs2.at[q_],
            device_id=(s, p, d), device_id_type=MESH)

    def go2(k, _):
        gather(ten(k), t).start()
        return 0

    def wr2(k, _):
        p = ten(k)
        gather(p, p).wait_recv()
        return 0

    lax.fori_loop(1, nt, go2, 0)
    locals_[2].wait()
    lax.fori_loop(1, nt, wr2, 0)

    tn = (((0,), (0,)), ((), ()))
    nt_dims = (((1,), (1,)), ((), ()))

    def grad_tile(r, half):
        cols = pl.ds(pl.multiple_of(half * 512, 512), 512)
        return lax.dot_general(
            aold[:, pl.ds(r * 256, 256)], gv[:, cols], tn, preferred_element_type=F32
        ) * (1.0 / 2048.0)

    for r in range(3):
        gsend[pl.ds(r * 256, 256)] = grad_tile(r, od).astype(BF)
    gcopy = pltpu.make_async_remote_copy(
        src_ref=gsend, dst_ref=grecv, send_sem=xss.at[1], recv_sem=xrs.at[1],
        device_id=dp_peer, device_id_type=MESH)
    gcopy.start()

    wcopy.wait_recv()

    def proj_tile(i, _):
        row = pl.multiple_of(i * 128, 128)
        a = aold[pl.ds(row, 128)]
        for h in range(2):
            r = jnp.dot(a, wf[h], preferred_element_type=F32)
            cols = pl.ds(h * 512, 512)
            lo, hi = r[:64], r[64:]
            pk[i, :, cols] = jnp.where(c == 0, hi, lo).astype(BF)
            pown[i, :, cols] = jnp.where(c == 0, lo, hi)
        return 0

    lax.fori_loop(0, nt, proj_tile, 0)
    ccopy = pltpu.make_async_remote_copy(
        src_ref=pk, dst_ref=cp, send_sem=xss.at[2], recv_sem=xrs.at[2],
        device_id=core_peer, device_id_type=MESH)
    ccopy.start()

    def hid(i):
        row = pl.multiple_of(i * 128, 128)
        r = lax.dot_general(gv[pl.ds(row, 128), pl.ds(0, 512)], wf[0], nt_dims, preferred_element_type=F32)
        return r + lax.dot_general(gv[pl.ds(row, 128), pl.ds(512, 512)], wf[1], nt_dims, preferred_element_type=F32)

    def hcopy(p, q_):
        return pltpu.make_async_remote_copy(
            src_ref=hgs.at[p], dst_ref=hgr.at[q_], send_sem=ssh.at[p], recv_sem=rsh.at[q_],
            device_id=(s, p, d), device_id_type=MESH)

    def go_h(k, _):
        p = ten(k)
        hgs[p] = hid(p).astype(BF)
        hcopy(p, t).start()
        return 0

    lax.fori_loop(1, nt, go_h, 0)
    hown = hid(t)
    for b in range(BLOCKS):
        hgr[t, :, pl.ds(b * 128, 128)] = hown[:, b * 128:(b + 1) * 128].astype(BF)

    for r in range(3):
        gown[pl.ds(r * 256, 256)] = grad_tile(r, d)

    ccopy.wait_recv()

    def qcopy(p, q_):
        return pltpu.make_async_remote_copy(
            src_ref=q.at[p], dst_ref=rq.at[q_], send_sem=ssq.at[p], recv_sem=rsq.at[q_],
            device_id=(p * 2 + c, t, d), device_id_type=MESH)

    def go_q(k, _):
        p = lax.rem(z + k, 8)
        q[p] = (pown[p] + cp[p].astype(F32)).astype(BF)
        qcopy(p, z).start()
        return 0

    lax.fori_loop(1, 8, go_q, 0)
    rq[z] = (pown[z] + cp[z].astype(F32)).astype(BF)

    locals_[3].wait()
    locals_[4].wait()
    gcopy.wait_recv()
    for b in range(BLOCKS):
        rows = pl.ds(b * 128, 128)
        g = gown[rows] + grecv[rows].astype(F32)
        f1 = 0.9 * fv[rows] + 0.1 * g
        s1 = 0.999 * sv[rows] + 0.001 * g * g
        ab[b] = (f1 / (jnp.sqrt(s1 / CORR_SECOND) + 1e-08)).astype(BF)
    go4, ws4, wr4 = to_sections(send4, recv4, ss4, rs4)
    for p in range(ns):
        send4[p] = ab[block_for[p]]
    go4()
    recv4[s] = send4[s]

    def wr_h(k, _):
        p = ten(k)
        hcopy(p, p).wait_recv()
        return 0

    lax.fori_loop(1, nt, wr_h, 0)
    for b in range(BLOCKS):
        acc = hgr[0, :, pl.ds(b * 128, 128)].astype(F32)
        for p in range(1, nt):
            acc = acc + hgr[p, :, pl.ds(b * 128, 128)].astype(F32)
        hb[b] = acc.astype(BF)
    for p in range(ns):
        send3[p] = hb[block_for[p]]
    go3, ws3, wr3 = to_sections(send3, recv3, ss3, rs3)
    go3()
    recv3[s] = send3[s]
    wr3()
    for k in range(RCAP):
        send5[k] = (recv3[owner_of[k]].astype(F32) * used[k]).astype(BF)

    def fcopy(p, q_):
        row = pl.multiple_of(q_ * 128, 128)
        return pltpu.make_async_remote_copy(
            src_ref=send5.at[p], dst_ref=hgf.at[pl.ds(row, 128)], send_sem=ss5.at[p], recv_sem=rs5.at[q_],
            device_id=(s, p, d), device_id_type=MESH)

    def go5(k, _):
        fcopy(ten(k), t).start()
        return 0

    def wr5(k, _):
        p = ten(k)
        fcopy(p, p).wait_recv()
        return 0

    lax.fori_loop(1, nt, go5, 0)
    hgf[pl.ds(trow, 128)] = send5[t]

    def wr_q(k, _):
        p = lax.rem(z + k, 8)
        qcopy(p, p).wait_recv()
        return 0

    lax.fori_loop(1, 8, wr_q, 0)
    acc = rq[0].astype(F32)
    for p in range(1, 8):
        acc = acc + rq[p].astype(F32)
    proj_out[...] = acc.astype(BF)

    lax.fori_loop(1, nt, wr5, 0)
    hidden_out[...] = hgf[...]

    wr4()
    for k in range(RCAP):
        step_out[pl.ds(k * 128, 128)] = recv4[owner_of[k]].astype(F32) * used[k]

    ws1()
    ws3()
    ws4()
    wcopy.wait_send()
    gcopy.wait_send()
    ccopy.wait_send()

    def ws_t(k, _):
        p = ten(k)
        gather(p, t).wait_send()
        hcopy(p, t).wait_send()
        fcopy(p, t).wait_send()
        return 0

    lax.fori_loop(1, nt, ws_t, 0)

    def ws_q(k, _):
        qcopy(lax.rem(z + k, 8), z).wait_send()
        return 0

    lax.fori_loop(1, 8, ws_q, 0)


def shards(old_master, old_first, old_second, dest_section, dest_offset, hidden_acts, out_grad):
    any_ = pl.BlockSpec(memory_space=pl.ANY)
    smem = pl.BlockSpec(memory_space=pltpu.SMEM)
    vmem = pl.BlockSpec(memory_space=pltpu.VMEM)
    V = pltpu.VMEM
    dma = pltpu.SemaphoreType.DMA
    tab = pl.pallas_call(
        plan,
        out_shape=jax.ShapeDtypeStruct((64,), jnp.int32),
        in_specs=[smem, smem],
        out_specs=smem,
        name="plan",
    )(dest_section, dest_offset)
    proj, hidden, step = pl.pallas_call(
        kernel,
        out_shape=(
            jax.ShapeDtypeStruct((64, 1024), BF),
            jax.ShapeDtypeStruct((1024, 128), BF),
            jax.ShapeDtypeStruct((1024, 512), F32),
        ),
        in_specs=[smem, any_, any_, any_, any_, any_],
        out_specs=(vmem, vmem, vmem),
        scratch_shapes=[
            V((128, 1024), BF), V((8, 128, 128), BF), V((768, 512), F32), V((1024, 1024), BF), V((768, 512), F32), V((768, 512), F32),
            V((16, 128, 128), BF), V((16, 128, 128), BF), V((1024, 768), BF), V((2, 768, 512), BF),
            V((768, 512), BF), V((768, 512), BF), V((768, 512), F32),
            V((8, 64, 1024), BF), V((8, 64, 1024), F32), V((8, 64, 1024), BF), V((8, 64, 1024), BF), V((8, 64, 1024), BF),
            V((8, 128, 768), BF), V((8, 128, 768), BF), V((6, 128, 128), BF), V((16, 128, 128), BF), V((16, 128, 128), BF),
            V((8, 128, 128), BF), V((1024, 128), BF), V((6, 128, 512), BF), V((16, 128, 512), BF), V((16, 128, 512), BF),
            dma((5,)), dma((16,)), dma((16,)), dma((8,)), dma((8,)), dma((3,)), dma((3,)), dma((8,)), dma((8,)),
            dma((8,)), dma((8,)), dma((16,)), dma((16,)), dma((8,)), dma((8,)), dma((16,)), dma((16,)),
        ],
        compiler_params=pltpu.CompilerParams(
            collective_id=0, has_side_effects=True, vmem_limit_bytes=56 * 2**20),
        name="layer",
    )(tab, old_master, old_first, old_second, hidden_acts[0], out_grad[0])
    return proj[None], hidden[None], step


def solution(mesh):
    placed = (
        P("section", ("tensor", "dp")),
        P("section", ("tensor", "dp")),
        P("section", ("tensor", "dp")),
        P(),
        P(),
        P("dp", None, "section"),
        P("dp", None, "tensor"),
    )
    return jax.shard_map(
        shards,
        mesh=mesh,
        in_specs=placed,
        out_specs=(
            P("dp", "section", "tensor"),
            P("dp", None, ("section", "tensor")),
            P("section", ("tensor", "dp")),
        ),
        check_vma=False,
    )
```

time: 480 us -> 156 us (0.33); the launches traced: 474 us -> 156 us
  waiting for transfers between devices: 340 us -> 0 us
  Pallas kernels: 0 us -> 149 us
  matrix products: 46.3 us -> 0 us
  local copies, waits for them, and re-layouts: 42.3 us -> 6.32 us
  starting transfers between devices: 23.7 us -> 0 us
  between operations: 14.1 us -> 0.65 us
  other arithmetic: 6.72 us -> 0 us
    all_to_all x3 -> x0, waiting for transfers between devices: 247 us -> none  [the longest x1 92.8 us: shards(): lax.all_to_all(packed(old_master), 'section', split_axis=0, concat_axis=0...]
    pallas_call x0 -> x2, Pallas kernels: none -> 149 us  [the longest x1 147 us: shards(): pl.pallas_call(kernel, out_shape=(jax.ShapeDtypeStruct((64, 1024), BF), j...]
    reduce_scatter x2 -> x0, waiting for transfers between devices: 79.6 us -> none  [the longest x1 79.6 us: shards(): lax.psum_scatter(partial_value, 'tensor', scatter_dimension=1, tiled=True)]
    dot_general x10 -> x0, matrix products: 46.3 us -> none  [the longest x3 20.1 us: placed(): jnp.dot(placing, received, precision=lax.Precision.HIGHEST)]
    all_to_all x3 -> x0, starting transfers between devices: 22.4 us -> none  [the longest x1 10.1 us: shards(): lax.all_to_all(packed(old_master), 'section', split_axis=0, concat_axis=0...]
    all_to_all x3 -> x0, local copies, waits for them, and re-layouts: 18.8 us -> none  [the longest x1 6.29 us: shards(): lax.all_to_all(packed(old_master), 'section', split_axis=0, concat_axis=0...]
    all_gather x1 -> x0, waiting for transfers between devices: 14.3 us -> none  [shards(): full_weight = lax.all_gather(weight, 'dp', axis=1, tiled=True)]
    reshape x3 -> x0, local copies, waits for them, and re-layouts: 9.31 us -> none  [packed(): state.reshape(BLOCKS, ROWS * width)]
  transfers between devices with their start and end apart: 7 -> 0, of which waited for: 5 -> 0; matrix products, arithmetic and copies ran while one was open for 15% -> 0% of each run, Pallas kernels for 0% -> 0%
where the time goes in v1:
time: 156 us
  Pallas kernels  149 us (96%)
  local copies, waits for them, and re-layouts  6.32 us (4%)
    pallas_call x1, Pallas kernels, shards(): pl.pallas_call(kernel, out_shape=(jax.ShapeDtypeStruct((64, 1024), BF), j...  147 us
    unnamed x3, local copies, waits for them, and re-layouts  6.32 us

profile of v1, /device:TPU:1, one launch (start us, length us, event | category | flops | bytes accessed | tf_op | source)
XLA Modules:
  0.0 156.0 jit_solution(16380494486689328371)
XLA Ops:
  0.6 1.7 %plan.1.tab = s32[64]{0:T(128)} custom-call(s32[96]{0:T(128)} %dest_ref.1, s32[96]{0:T(128)} %off_ref.1), custom_call_target="tpu_custom_call" | custom-call | tf_op jit(solution)/shard_map/plan/pallas_call | solution.py:335
  2.3 147.3 %layer.1 = (bf16[64,1024]{1,0:T(8,128)(2,1)}, bf16[1024,128]{1,0:T(8,128)(2,1)}, f32[1024,512]{1,0:T(8,128)}) custom-call(s32[64]{0:T(128)} %plan.1.tab, f32[768,512]{1,0:T(8,128)} %master.1, f32[768,512]{1,0:T(8,128)} %first.1, f32[768,512]{1,0:T(8,128)} %second.1, bf16[1024,1024]{1,0:T(8,128)(2,1)} %bitcast.4, bf16[1024,1024]{1,0:T(8,128)(2,1)} %bitcast.5), custom_call_target="tpu_custom_call" | custom-call | tf_op jit(solution)/shard_map/layer/pallas_call | solution.py:342
  149.7 1.6 %copy.13 = bf16[1,64,1024]{2,1,0:T(8,128)(2,1)} copy(bf16[1,64,1024]{2,1,0:T(8,128)(2,1)} %bitcast.7) | data formatting | bytes 262144
  151.2 1.7 %copy.14 = bf16[1,1024,128]{2,1,0:T(8,128)(2,1)} copy(bf16[1,1024,128]{2,1,0:T(8,128)(2,1)} %bitcast.6) | data formatting | bytes 524288
  152.9 3.1 %copy.15 = f32[1024,512]{1,0:T(8,128)} copy(f32[1024,512]{1,0:T(8,128)} %get-tuple-element.14) | data formatting | bytes 4194304

commit v2 on v1

--- a/solution.py
+++ b/solution.py
@@ -14,18 +14,26 @@
 F32 = jnp.float32
 
 
-def plan(dest_ref, off_ref, tab):
+def plan(dest, off, tab, route):
     s = lax.axis_index("section")
-    for i in range(64):
-        tab[i] = 0
+    z = s // 2
+    for i in range(128):
+        tab[i] = 30 if 80 <= i < 96 else (8 if 64 <= i < 74 else (1 if i == 96 else 0))
+
+    def clear(i, _):
+        for j in range(8):
+            route[i * 8 + j] = -1
+        return 0
+
+    lax.fori_loop(0, 32, clear, 0)
 
     def owner(o, _):
         for b in range(BLOCKS):
             g = o * BLOCKS + b
 
-            @pl.when(dest_ref[g] == s)
+            @pl.when(dest[g] == s)
             def _():
-                k = off_ref[g]
+                k = off[g]
                 tab[o] = k
                 tab[32 + k] = o
                 tab[40 + k] = 1
@@ -34,12 +42,104 @@
 
     lax.fori_loop(0, 16, owner, 0)
     for b in range(BLOCKS):
-        p = dest_ref[s * BLOCKS + b]
+        p = dest[s * BLOCKS + b]
         tab[16 + p] = b
         tab[48 + b] = p
 
-
-def kernel(
+    def rank(a, _):
+        count = jnp.int32(0)
+        for i in range(12):
+            g = a * 12 + i
+            p = dest[g] // 2
+            r = jnp.bitwise_and(lax.shift_right_logical(count, p * 4), 15)
+            count = count + lax.shift_left(jnp.int32(1), p * 4)
+            route[r * 64 + a * 8 + p] = g
+        return 0
+
+    lax.fori_loop(0, 8, rank, 0)
+
+    def near(a, p):
+        k = jnp.bitwise_and(p - a, 7)
+        return (k == 1) | (k == 7)
+
+    def detour(a, p, g):
+        best = jnp.int32(-1)
+        for k in (4, 3, 5, 2, 6, 1, 7):
+            m = jnp.bitwise_and(p + k, 7)
+            am, mp = a * 8 + m, m * 8 + p
+            last = jnp.where(route[64 + mp] < 0, 1, jnp.where((k == 1 or k == 7) & (route[128 + mp] < 0), 2, 0))
+            held = route[am]
+            direct = dest[jnp.maximum(held, 0)] // 2 == m
+            second = jnp.where(route[64 + am] < 0, 1, jnp.where(near(a, m) & (route[128 + am] < 0), 2, 3))
+            move = jnp.where(held < 0, 0, jnp.where(direct, second, 3))
+            good = (last > 0) & (move < 3) & (m != a)
+            best = jnp.where(good, m * 16 + last * 4 + move, best)
+
+        @pl.when(best >= 0)
+        def _():
+            m = best // 16
+            am = a * 8 + m
+            move = jnp.bitwise_and(best, 3)
+            last = jnp.bitwise_and(best // 4, 3)
+
+            @pl.when(move > 0)
+            def _():
+                route[move * 64 + am] = route[am]
+
+            route[am] = g
+            route[last * 64 + m * 8 + p] = g
+
+        @pl.when(best < 0)
+        def _():
+            tab[96] = 0
+
+    def spill(pair, _):
+        a, p = pair // 8, jnp.bitwise_and(pair, 7)
+        g2, g3 = route[128 + pair], route[192 + pair]
+
+        @pl.when((a != p) & (g2 >= 0) & jnp.logical_not(near(a, p)))
+        def _():
+            route[128 + pair] = -1
+            detour(a, p, g2)
+
+        @pl.when((a != p) & (g3 >= 0))
+        def _():
+            detour(a, p, g3)
+
+        return 0
+
+    lax.fori_loop(0, 64, spill, 0)
+
+    for m in range(8):
+        g = route[z * 8 + m]
+        tab[56 + m] = jnp.where((g >= 0) & (z != m), g - 12 * z, 0)
+    for j in range(10):
+        if j < 8:
+            g = route[64 + z * 8 + j]
+        else:
+            g = route[128 + z * 8 + jnp.bitwise_and(z + (1 if j == 8 else 7), 7)]
+        a = jnp.maximum(g, 0) // 12
+        from_pool = 8 + g - 12 * z
+        tab[64 + j] = jnp.where(g < 0, 8, jnp.where(a == z, from_pool, a))
+
+    def final(g, source, wanted):
+        h = jnp.maximum(g, 0)
+        p = dest[h]
+
+        @pl.when(wanted & (g >= 0) & (p // 2 == z))
+        def _():
+            tab[80 + jnp.bitwise_and(p, 1) * 8 + off[h]] = source
+
+    for a in range(8):
+        final(route[a * 8 + z], 8 + a, a != z)
+        final(route[64 + a * 8 + z], a, a != z)
+    final(route[128 + jnp.bitwise_and(z + 7, 7) * 8 + z], 28, True)
+    final(route[128 + jnp.bitwise_and(z + 1, 7) * 8 + z], 29, True)
+    for l in range(12):
+        final(12 * z + l, 16 + l, True)
+
+
+def padded_kernel(
     tab, master, first, second, acts, grads,
     proj_out, hidden_out, step_out,
     strip, blk, mv, gv, fv, sv,
@@ -301,7 +401,7 @@
 
     wr4()
     for k in range(RCAP):
-        step_out[pl.ds(k * 128, 128)] = recv4[owner_of[k]].astype(F32) * used[k]
+        step_out[k] = (recv4[owner_of[k]].astype(F32) * used[k]).astype(BF)
 
     ws1()
     ws3()
@@ -324,6 +424,396 @@
         return 0
 
     lax.fori_loop(1, 8, ws_q, 0)
+
+
+def routed_kernel(
+    tab, master, first, second, acts, grads,
+    proj_out, hidden_out, step_out,
+    strip, blk, mv, gv, fv, sv,
+    send1, recv1, aold, wf, gq, gsend, grecv, gown, pk, pown, cp, q, rq,
+    hgs, hgr, hxs, hxr, hown, send5, hgf,
+    ab0, pool0, xa0, fa0, sa0, sb0, xs0, xr0,
+    ab1, pool1, xa1, fa1, sa1, sb1, xs1, xr1,
+    ab2, pool2, xa2, fa2, sa2, sb2, xs2, xr2,
+    lsem, ss1, rs1, ss2, rs2, xss, xrs, ssq, rsq, ssh, rsh, ss5, rs5, rss, rsr,
+):
+    ns, nt = 16, 8
+    s = lax.axis_index("section")
+    t = lax.axis_index("tensor")
+    d = lax.axis_index("dp")
+    z, c = s // 2, s % 2
+    y, xl = t // 2, t % 2
+    od, oc, tx = 1 - d, 1 - c, y * 2 + (1 - xl)
+    core_peer = (z * 2 + oc, t, d)
+    dp_peer = (s, t, od)
+    x_peer = (s, tx, d)
+
+    def sec(k):
+        return lax.rem(s + k, ns)
+
+    def ten(k):
+        return lax.rem(t + k, nt)
+
+    def ypeer(k):
+        return lax.rem(y + k, 4)
+
+    def chip(k):
+        return lax.rem(z + k, 8)
+
+    def remote(src, dst, sends, recvs, device):
+        return pltpu.make_async_remote_copy(
+            src_ref=src, dst_ref=dst, send_sem=sends, recv_sem=recvs,
+            device_id=device, device_id_type=MESH)
+
+    trow = pl.multiple_of(t * 128, 128)
+    xrow = pl.multiple_of(tx * 128, 128)
+    locals_ = [
+        pltpu.make_async_copy(acts.at[pl.ds(trow, 128)], strip, lsem.at[0]),
+        pltpu.make_async_copy(master, mv, lsem.at[1]),
+        pltpu.make_async_copy(grads, gv, lsem.at[2]),
+        pltpu.make_async_copy(first, fv, lsem.at[3]),
+        pltpu.make_async_copy(second, sv, lsem.at[4]),
+    ]
+    for cpy in locals_:
+        cpy.start()
+
+    bar = pltpu.get_barrier_semaphore()
+    for k in range(1, ns):
+        pl.semaphore_signal(bar, inc=1, device_id=(sec(k), t, d), device_id_type=MESH)
+    for k in range(1, nt):
+        pl.semaphore_signal(bar, inc=1, device_id=(s, ten(k), d), device_id_type=MESH)
+    pl.semaphore_signal(bar, inc=1, device_id=dp_peer, device_id_type=MESH)
+
+    locals_[0].wait()
+    for k in range(RCAP):
+        blk[k] = strip[:, pl.ds(k * 128, 128)]
+    for o in range(ns):
+        send1[o] = blk[tab[o]]
+    locals_[1].wait()
+    for b in range(BLOCKS):
+        wf[d, pl.ds(b * 128, 128)] = mv[pl.ds(b * 128, 128)].astype(BF)
+
+    pl.semaphore_wait(bar, ns - 1 + nt - 1 + 1)
+
+    def acopy(p, o):
+        return remote(send1.at[p], recv1.at[o], ss1.at[p], rs1.at[o], (p, t, d))
+
+    def go1(k, _):
+        acopy(sec(k), s).start()
+        return 0
+
+    lax.fori_loop(1, ns, go1, 0)
+    wcopy = remote(wf.at[d], wf.at[d], xss.at[0], xrs.at[0], dp_peer)
+    wcopy.start()
+    recv1[s] = send1[s]
+
+    locals_[2].wait()
+    for u in range(2):
+        for j in range(2):
+            src = j * 256 + u * 128
+            for h in range(2):
+                gq[h, u, :, pl.ds(j * 128, 128)] = gv[:, pl.ds(h * 512 + src, 128)]
+
+    def wr1(k, _):
+        p = sec(k)
+        acopy(p, p).wait_recv()
+        return 0
+
+    lax.fori_loop(1, ns, wr1, 0)
+    for b in range(BLOCKS):
+        aold[pl.ds(trow, 128), pl.ds(b * 128, 128)] = recv1[tab[48 + b]]
+
+    def piece(i, sends, owner, device):
+        rows = aold.at[pl.ds(pl.multiple_of(owner * 128, 128), 128)]
+        return remote(rows, rows, ss2.at[sends], rs2.at[owner], device)
+
+    gx = piece(0, 0, t, x_peer)
+    gx.start()
+    for k in range(1, 4):
+        piece(0, k, t, (s, ypeer(k) * 2 + xl, d)).start()
+    piece(0, 0, tx, x_peer).wait_recv()
+    for k in range(1, 4):
+        piece(0, 3 + k, tx, (s, ypeer(k) * 2 + xl, d)).start()
+
+    nt_dims = (((1,), (1,)), ((), ()))
+    tn = (((0,), (0,)), ((), ()))
+    wcopy.wait_recv()
+
+    def hid(i):
+        row = pl.multiple_of(i * 128, 128)
+        r = lax.dot_general(gv[pl.ds(row, 128), pl.ds(0, 512)], wf[0], nt_dims, preferred_element_type=F32)
+        return r + lax.dot_general(gv[pl.ds(row, 128), pl.ds(512, 512)], wf[1], nt_dims, preferred_element_type=F32)
+
+    def hid_y(k, _):
+        i = ypeer(k)
+        for x in range(2):
+            hgs[i, x] = hid(i * 2 + x).astype(BF)
+        return 0
+
+    lax.fori_loop(1, 4, hid_y, 0)
+    for x in range(2):
+        hown[x] = hid(y * 2 + x)
+
+    for k in range(1, 4):
+        piece(0, 0, ypeer(k) * 2 + xl, x_peer).wait_recv()
+        piece(0, 0, ypeer(k) * 2 + (1 - xl), x_peer).wait_recv()
+
+    def grad_tile(r, h, u):
+        return lax.dot_general(
+            aold[:, pl.ds(r * 256, 256)], gq[h, u], tn, preferred_element_type=F32) * (1.0 / 2048.0)
+
+    gcopies = []
+    for u in range(2):
+        for r in range(3):
+            gsend[u, pl.ds(r * 256, 256)] = grad_tile(r, od, u).astype(BF)
+        gcopies.append(remote(gsend.at[u], grecv.at[u], xss.at[1 + u], xrs.at[1 + u], dp_peer))
+        gcopies[u].start()
+
+    def hcopy(i, o):
+        return remote(hgs.at[i], hgr.at[o], ssh.at[i], rsh.at[o], (s, i * 2 + xl, d))
+
+    for k in range(1, 4):
+        hcopy(ypeer(k), y).start()
+
+    def proj_tile(i, _):
+        a = aold[pl.ds(pl.multiple_of(i * 128, 128), 128)]
+        for h in range(2):
+            r = jnp.dot(a, wf[h], preferred_element_type=F32)
+            cols = pl.ds(h * 512, 512)
+            lo, hi = r[:64], r[64:]
+            pk[i, :, cols] = jnp.where(c == 0, hi, lo).astype(BF)
+            pown[i, :, cols] = jnp.where(c == 0, lo, hi)
+        return 0
+
+    lax.fori_loop(0, nt, proj_tile, 0)
+    ccopy = remote(pk, cp, xss.at[3], xrs.at[3], core_peer)
+    ccopy.start()
+
+    for u in range(2):
+        for r in range(3):
+            gown[u, pl.ds(r * 256, 256)] = grad_tile(r, d, u)
+
+    ccopy.wait_recv()
+
+    def qcopy(p, o):
+        return remote(q.at[p], rq.at[o], ssq.at[p], rsq.at[o], (p * 2 + c, t, d))
+
+    def go_q(k, _):
+        p = chip(k)
+        q[p] = (pown[p] + cp[p].astype(F32)).astype(BF)
+        qcopy(p, z).start()
+        return 0
+
+    lax.fori_loop(1, 8, go_q, 0)
+    rq[z] = (pown[z] + cp[z].astype(F32)).astype(BF)
+
+    parts = [
+        (ab0, pool0, xa0, fa0, sa0, sb0, xs0, xr0),
+        (ab1, pool1, xa1, fa1, sa1, sb1, xs1, xr1),
+        (ab2, pool2, xa2, fa2, sa2, sb2, xs2, xr2),
+    ]
+
+    def swap_copy(u):
+        ab_, pool_ = parts[u][:2]
+        return remote(ab_.at[oc], pool_.at[pl.ds(c * BLOCKS, BLOCKS)], rss.at[u, 0], rsr.at[u, 0], core_peer)
+
+    def enter(u):
+        ab_, pool_ = parts[u][:2]
+        swap_copy(u).start()
+        for b in range(BLOCKS):
+            pool_[c * BLOCKS + b] = ab_[c, b]
+
+    def copy_a(u, p, o):
+        return remote(parts[u][4].at[p], parts[u][2].at[o], rss.at[u, 1 + p], rsr.at[u, 1 + o], (p * 2 + c, t, d))
+
+    def copy_b(u, p, o):
+        return remote(parts[u][5].at[p], parts[u][3].at[o], rss.at[u, 9 + p], rsr.at[u, 9 + o], (p * 2 + c, t, d))
+
+    def copy_n(u, j):
+        p = chip(1 if j == 0 else 7)
+        return remote(parts[u][5].at[8 + j], parts[u][3].at[28 + j], rss.at[u, 17 + j], rsr.at[u, 17 + j], (p * 2 + c, t, d))
+
+    order = (4, 3, 5, 2, 6, 1, 7)
+
+    def round_a(u):
+        _, pool_, xa_, _, sa_, _, _, _ = parts[u]
+        swap_copy(u).wait_recv()
+        for k in order:
+            m = chip(k)
+            sa_[m] = pool_[tab[56 + m]]
+            copy_a(u, m, z).start()
+        for l in range(12):
+            xa_[8 + l] = pool_[l]
+        xa_[z] = jnp.zeros(xa_.shape[1:], BF)
+
+    def round_b(u):
+        _, pool_, xa_, fa_, _, sb_, _, _ = parts[u]
+        for k in order:
+            m = chip(k)
+            copy_a(u, m, m).wait_recv()
+        for k in order:
+            m = chip(k)
+            sb_[m] = xa_[tab[64 + m]]
+            copy_b(u, m, z).start()
+        for j in range(2):
+            sb_[8 + j] = xa_[tab[72 + j]]
+            copy_n(u, j).start()
+        for l in range(20):
+            fa_[8 + l] = xa_[l]
+        fa_[z] = jnp.zeros(fa_.shape[1:], BF)
+        fa_[30] = jnp.zeros(fa_.shape[1:], BF)
+
+    def back_copy(u):
+        return remote(parts[u][6], parts[u][7], rss.at[u, 19], rsr.at[u, 19], core_peer)
+
+    def arrive(u):
+        _, _, _, fa_, _, _, xs_, _ = parts[u]
+        for k in order:
+            m = chip(k)
+            copy_b(u, m, m).wait_recv()
+        for j in range(2):
+            copy_n(u, j).wait_recv()
+        for k in range(RCAP):
+            xs_[k] = fa_[tab[80 + oc * 8 + k]]
+        back_copy(u).start()
+
+    def drain(u):
+        swap_copy(u).wait_send()
+        back_copy(u).wait_send()
+        for k in order:
+            copy_a(u, chip(k), z).wait_send()
+            copy_b(u, chip(k), z).wait_send()
+        for j in range(2):
+            copy_n(u, j).wait_send()
+
+    def adam(u):
+        gcopies[u].wait_recv()
+        for b in range(BLOCKS):
+            rows = pl.ds(b * 128, 128)
+            for j in range(2):
+                cols = pl.ds(j * 256 + u * 128, 128)
+                here = pl.ds(j * 128, 128)
+                g = gown[u, rows, here] + grecv[u, rows, here].astype(F32)
+                f1 = 0.9 * fv[rows, cols] + 0.1 * g
+                s1 = 0.999 * sv[rows, cols] + 0.001 * g * g
+                parts[u][0][j, b] = (f1 / (jnp.sqrt(s1 / CORR_SECOND) + 1e-08)).astype(BF)
+        enter(u)
+
+    def place(u):
+        fa_, xr_ = parts[u][3], parts[u][7]
+        back_copy(u).wait_recv()
+        mine = pl.ds(pl.multiple_of(c * 256 + u * 128, 128), 128)
+        theirs = pl.ds(pl.multiple_of(oc * 256 + u * 128, 128), 128)
+        for k in range(RCAP):
+            step_out[k, :, mine] = fa_[tab[80 + c * 8 + k]]
+            step_out[k, :, theirs] = xr_[k]
+
+    locals_[3].wait()
+    locals_[4].wait()
+    adam(0)
+    round_a(0)
+    adam(1)
+
+    for k in range(1, 4):
+        p = ypeer(k)
+        hcopy(p, p).wait_recv()
+    for x in range(2):
+        total = hown[x]
+        for k in range(1, 4):
+            total = total + hgr[ypeer(k), x].astype(F32)
+        hown[x] = total
+    hxs[...] = hown[1 - xl].astype(BF)
+    hx = remote(hxs, hxr, xss.at[4], xrs.at[4], x_peer)
+    hx.start()
+
+    round_a(1)
+    round_b(0)
+    hx.wait_recv()
+    hsum = hown[xl] + hxr[...].astype(F32)
+    for b in range(BLOCKS):
+        piece_ = hsum[:, b * 128:(b + 1) * 128].astype(BF)
+        for j in range(2):
+            ab2[j, b] = piece_[j * 64:(j + 1) * 64]
+    enter(2)
+    round_a(2)
+    round_b(1)
+    round_b(2)
+    arrive(0)
+    place(0)
+    arrive(1)
+    arrive(2)
+
+    back_copy(2).wait_recv()
+    mine = pl.ds(pl.multiple_of(c * 64, 64), 64)
+    theirs = pl.ds(pl.multiple_of(oc * 64, 64), 64)
+    for k in range(RCAP):
+        send5[k, mine] = fa2[tab[80 + c * 8 + k]]
+        send5[k, theirs] = xr2[k]
+
+    def fcopy(p, o):
+        rows = pl.ds(pl.multiple_of(o * 128, 128), 128)
+        return remote(send5.at[p], hgf.at[rows], ss5.at[p], rs5.at[o], (s, p, d))
+
+    def go5(k, _):
+        fcopy(ten(k), t).start()
+        return 0
+
+    lax.fori_loop(1, nt, go5, 0)
+    hgf[pl.ds(trow, 128)] = send5[t]
+    place(1)
+
+    def wr_q(k, _):
+        p = chip(k)
+        qcopy(p, p).wait_recv()
+        return 0
+
+    lax.fori_loop(1, 8, wr_q, 0)
+    acc = rq[0].astype(F32)
+    for p in range(1, 8):
+        acc = acc + rq[p].astype(F32)
+    proj_out[...] = acc.astype(BF)
+
+    def wr5(k, _):
+        p = ten(k)
+        fcopy(p, p).wait_recv()
+        return 0
+
+    lax.fori_loop(1, nt, wr5, 0)
+    hidden_out[...] = hgf[...]
+
+    for u in range(3):
+        drain(u)
+    for cpy in (wcopy, gcopies[0], gcopies[1], ccopy, hx, gx):
+        cpy.wait_send()
+    for k in range(1, 4):
+        piece(0, k, t, x_peer).wait_send()
+        piece(0, 3 + k, tx, x_peer).wait_send()
+        hcopy(ypeer(k), y).wait_send()
+
+    def ws(k, _):
+        acopy(sec(k), s).wait_send()
+        return 0
+
+    lax.fori_loop(1, ns, ws, 0)
+
+    def ws5(k, _):
+        fcopy(ten(k), t).wait_send()
+        return 0
+
+    lax.fori_loop(1, nt, ws5, 0)
+
+    def ws_q(k, _):
+        qcopy(chip(k), z).wait_send()
+        return 0
+
+    lax.fori_loop(1, 8, ws_q, 0)
+
+
+def finish(proj, hidden, step, proj_out, hidden_out, step_out):
+    proj_out[...] = proj[...]
+    hidden_out[...] = hidden[...]
+    for k in range(RCAP):
+        step_out[pl.ds(k * 128, 128)] = step[k].astype(F32)
 
 
 def shards(old_master, old_first, old_second, dest_section, dest_offset, hidden_acts, out_grad):
@@ -334,34 +824,72 @@
     dma = pltpu.SemaphoreType.DMA
     tab = pl.pallas_call(
         plan,
-        out_shape=jax.ShapeDtypeStruct((64,), jnp.int32),
+        out_shape=jax.ShapeDtypeStruct((128,), jnp.int32),
         in_specs=[smem, smem],
         out_specs=smem,
+        scratch_shapes=[pltpu.SMEM((256,), jnp.int32)],
         name="plan",
     )(dest_section, dest_offset)
+    out_shape = (
+        jax.ShapeDtypeStruct((64, 1024), BF),
+        jax.ShapeDtypeStruct((1024, 128), BF),
+        jax.ShapeDtypeStruct((8, 128, 512), BF),
+    )
+
+    def call(body, scratch, number, name):
+        return pl.pallas_call(
+            body,
+            out_shape=out_shape,
+            in_specs=[smem, any_, any_, any_, any_, any_],
+            out_specs=(vmem, vmem, vmem),
+            scratch_shapes=scratch,
+            compiler_params=pltpu.CompilerParams(
+                collective_id=number, has_side_effects=True, vmem_limit_bytes=58 * 2**20),
+            name=name,
+        )
+
+    padded = call(padded_kernel, [
+        V((128, 1024), BF), V((8, 128, 128), BF), V((768, 512), F32), V((1024, 1024), BF), V((768, 512), F32), V((768, 512), F32),
+        V((16, 128, 128), BF), V((16, 128, 128), BF), V((1024, 768), BF), V((2, 768, 512), BF),
+        V((768, 512), BF), V((768, 512), BF), V((768, 512), F32),
+        V((8, 64, 1024), BF), V((8, 64, 1024), F32), V((8, 64, 1024), BF), V((8, 64, 1024), BF), V((8, 64, 1024), BF),
+        V((8, 128, 768), BF), V((8, 128, 768), BF), V((6, 128, 128), BF), V((16, 128, 128), BF), V((16, 128, 128), BF),
+        V((8, 128, 128), BF), V((1024, 128), BF), V((6, 128, 512), BF), V((16, 128, 512), BF), V((16, 128, 512), BF),
+        dma((5,)), dma((16,)), dma((16,)), dma((8,)), dma((8,)), dma((3,)), dma((3,)), dma((8,)), dma((8,)),
+        dma((8,)), dma((8,)), dma((16,)), dma((16,)), dma((8,)), dma((8,)), dma((16,)), dma((16,)),
+    ], 0, "padded")
+
+
+    def buffers(rows):
+        shapes = ((2, 6), (12,), (20,), (31,), (8,), (10,), (8,), (8,))
+        return [V((*n, rows, 128), BF) for n in shapes]
+
+    routed = call(routed_kernel, [
+        V((128, 1024), BF), V((8, 128, 128), BF), V((768, 512), F32), V((1024, 1024), BF), V((768, 512), F32), V((768, 512), F32),
+        V((16, 128, 128), BF), V((16, 128, 128), BF), V((1024, 768), BF), V((2, 768, 512), BF),
+        V((2, 2, 1024, 256), BF), V((2, 768, 256), BF), V((2, 768, 256), BF), V((2, 768, 256), F32),
+        V((8, 64, 1024), BF), V((8, 64, 1024), F32), V((8, 64, 1024), BF), V((8, 64, 1024), BF), V((8, 64, 1024), BF),
+        V((4, 2, 128, 768), BF), V((4, 2, 128, 768), BF), V((128, 768), BF), V((128, 768), BF), V((2, 128, 768), F32),
+        V((8, 128, 128), BF), V((1024, 128), BF),
+        *buffers(128), *buffers(128), *buffers(64),
+        dma((5,)), dma((16,)), dma((16,)), dma((8,)), dma((8,)), dma((5,)), dma((5,)), dma((8,)), dma((8,)),
+        dma((4,)), dma((4,)), dma((8,)), dma((8,)), dma((3, 20)), dma((3, 20)),
+    ], 1, "routed")
+
+    args = (tab, old_master, old_first, old_second, hidden_acts[0], out_grad[0])
+    proj, hidden, step = lax.cond(tab[96] == 1, routed, padded, *args)
     proj, hidden, step = pl.pallas_call(
-        kernel,
+        finish,
         out_shape=(
             jax.ShapeDtypeStruct((64, 1024), BF),
             jax.ShapeDtypeStruct((1024, 128), BF),
             jax.ShapeDtypeStruct((1024, 512), F32),
         ),
-        in_specs=[smem, any_, any_, any_, any_, any_],
+        in_specs=[vmem] * 3,
         out_specs=(vmem, vmem, vmem),
-        scratch_shapes=[
-            V((128, 1024), BF), V((8, 128, 128), BF), V((768, 512), F32), V((1024, 1024), BF), V((768, 512), F32), V((768, 512), F32),
-            V((16, 128, 128), BF), V((16, 128, 128), BF), V((1024, 768), BF), V((2, 768, 512), BF),
-            V((768, 512), BF), V((768, 512), BF), V((768, 512), F32),
-            V((8, 64, 1024), BF), V((8, 64, 1024), F32), V((8, 64, 1024), BF), V((8, 64, 1024), BF), V((8, 64, 1024), BF),
-            V((8, 128, 768), BF), V((8, 128, 768), BF), V((6, 128, 128), BF), V((16, 128, 128), BF), V((16, 128, 128), BF),
-            V((8, 128, 128), BF), V((1024, 128), BF), V((6, 128, 512), BF), V((16, 128, 512), BF), V((16, 128, 512), BF),
-            dma((5,)), dma((16,)), dma((16,)), dma((8,)), dma((8,)), dma((3,)), dma((3,)), dma((8,)), dma((8,)),
-            dma((8,)), dma((8,)), dma((16,)), dma((16,)), dma((8,)), dma((8,)), dma((16,)), dma((16,)),
-        ],
-        compiler_params=pltpu.CompilerParams(
-            collective_id=0, has_side_effects=True, vmem_limit_bytes=56 * 2**20),
-        name="layer",
-    )(tab, old_master, old_first, old_second, hidden_acts[0], out_grad[0])
+        compiler_params=pltpu.CompilerParams(vmem_limit_bytes=32 * 2**20),
+        name="finish",
+    )(proj, hidden, step)
     return proj[None], hidden[None], step
 
 

time: 156 us -> 124 us (0.79)
  Pallas kernels: 149 us -> 122 us
  local copies, waits for them, and re-layouts: 6.32 us -> 0.58 us
    pallas_call x2 -> x3, Pallas kernels: 149 us -> 122 us  [the longest x1 115 us: shards(): proj, hidden, step = lax.cond(tab[96] == 1, routed, padded, *args)]
    unnamed x3 -> x0, local copies, waits for them, and re-layouts: 6.32 us -> none
where the time goes in v2:
time: 124 us
  Pallas kernels  122 us (98%)
  between operations  1.3 us (1%)
    pallas_call x1, Pallas kernels, shards(): proj, hidden, step = lax.cond(tab[96] == 1, routed, padded, *args)  115 us
    pallas_call x1, Pallas kernels, shards(): pl.pallas_call(plan, out_shape=jax.ShapeDtypeStruct((128,), jnp.int32), i...  5.21 us

profile of v2, /device:TPU:1, one launch (start us, length us, event | category | flops | bytes accessed | tf_op | source)
XLA Modules:
  0.0 123.9 jit_solution(1363569868484813768)
XLA Ops:
  0.6 5.2 %plan.1 = s32[128]{0:T(128)S(1)} custom-call(s32[96]{0:T(128)} %dest.1, s32[96]{0:T(128)} %off.1), custom_call_target="tpu_custom_call" | custom-call | tf_op jit(solution)/shard_map/plan/pallas_call | solution.py:825
  5.8 0.6 slice.3
  7.1 115.2 %conditional.1 = ((bf16[64,1024]{1,0:T(8,128)(2,1)S(1)}, bf16[1024,128]{1,0:T(8,128)(2,1)S(1)}, bf16[8,128,512]{2,1,0:T(8,128)(2,1)S(1)})) conditional(s32[]{:T(128)} %bitcast, (s32[128]{0:T(128)S(1)}, f32[768,512]{1,0:T(8,128)}, f32[768,512]{1,0:T(8,128)}, f32[768,512]{1,0:T(8,128)}, bf16[1024,1024]{1,0:T(8,128)(2,1)}, ...), branch_computations={%region_0.0_spmd, %region_1.0_spmd} | conditional | bytes 8 | solution.py:880
  7.3 115.0 %routed.1 = (bf16[64,1024]{1,0:T(8,128)(2,1)S(1)}, bf16[1024,128]{1,0:T(8,128)(2,1)S(1)}, bf16[8,128,512]{2,1,0:T(8,128)(2,1)S(1)}) custom-call(s32[128]{0:T(128)S(1)} %get-tuple-element.30.tab, f32[768,512]{1,0:T(8,128)} %get-tuple-element.31.master, f32[768,512]{1,0:T(8,128)} %get-tuple-element.32.first, f32[768,512]{1,0:T(8,128)} %get-tuple-element.33.second, ...), custom_call_target="tpu_custom_call" | custom-call | tf_op jit(solution)/shard_map/cond/branch_1_fun/routed/pallas_call | solution.py:880
  122.3 1.6 %finish.1 = (bf16[64,1024]{1,0:T(8,128)(2,1)}, bf16[1024,128]{1,0:T(8,128)(2,1)}, f32[1024,512]{1,0:T(8,128)}) custom-call(bf16[64,1024]{1,0:T(8,128)(2,1)S(1)} %get-tuple-element.45.proj, bf16[1024,128]{1,0:T(8,128)(2,1)S(1)} %get-tuple-element.46.hidden, bf16[8,128,512]{2,1,0:T(8,128)(2,1)S(1)} %get-tuple-element.47.step), custom_call_target="tpu_custom_call" | custom-call | tf_op jit(solution)/shard_map/finish/pallas_call | solution.py:881

commit v3 on v2

--- a/solution.py
+++ b/solution.py
@@ -14,62 +14,62 @@
 F32 = jnp.float32
 
 
-def plan(dest, off, tab, route):
+def plan(dest, off, tab, ok, route, late):
     s = lax.axis_index("section")
     z = s // 2
-    for i in range(128):
-        tab[i] = 30 if 80 <= i < 96 else (8 if 64 <= i < 74 else (1 if i == 96 else 0))
+    for i in range(112):
+        tab[i] = 30 if 80 <= i < 96 else (8 if 64 <= i < 74 else 0)
+    ok[0] = 1
 
     def clear(i, _):
-        for j in range(8):
-            route[i * 8 + j] = -1
-        return 0
-
-    lax.fori_loop(0, 32, clear, 0)
-
-    def owner(o, _):
-        for b in range(BLOCKS):
-            g = o * BLOCKS + b
-
-            @pl.when(dest[g] == s)
-            def _():
-                k = off[g]
-                tab[o] = k
-                tab[32 + k] = o
-                tab[40 + k] = 1
-
-        return 0
-
-    lax.fori_loop(0, 16, owner, 0)
+        for j in range(16):
+            route[i * 16 + j] = -1
+        return 0
+
+    lax.fori_loop(0, 12, clear, 0)
+
+    def near(a, p):
+        k = jnp.bitwise_and(p - a, 7)
+        return (k == 1) | (k == 7)
+
+    def rank(a, n):
+        count = jnp.int32(0)
+        for i in range(12):
+            g = a * 12 + i
+            o = a * 2 + i // 6
+            q = dest[g]
+            k = off[g]
+            here = q == s
+            tab[jnp.where(here, o, 112)] = k
+            tab[jnp.where(here, 32 + k, 113)] = o
+            tab[jnp.where(here, 40 + k, 114)] = 1
+            p = lax.shift_right_logical(q, 1)
+            r = jnp.bitwise_and(lax.shift_right_logical(count, p * 4), 15)
+            count = count + lax.shift_left(jnp.int32(1), p * 4)
+            fits = (r < 2) | ((r == 2) & near(a, p)) | (a == p)
+            route[jnp.where(fits & (a != p), r * 64 + a * 8 + p, 192)] = g
+            late[n] = g
+            n = n + jnp.where(fits, 0, 1)
+        return n
+
+    n_late = lax.fori_loop(0, 8, rank, jnp.int32(0))
     for b in range(BLOCKS):
         p = dest[s * BLOCKS + b]
         tab[16 + p] = b
         tab[48 + b] = p
 
-    def rank(a, _):
-        count = jnp.int32(0)
-        for i in range(12):
-            g = a * 12 + i
-            p = dest[g] // 2
-            r = jnp.bitwise_and(lax.shift_right_logical(count, p * 4), 15)
-            count = count + lax.shift_left(jnp.int32(1), p * 4)
-            route[r * 64 + a * 8 + p] = g
-        return 0
-
-    lax.fori_loop(0, 8, rank, 0)
-
-    def near(a, p):
-        k = jnp.bitwise_and(p - a, 7)
-        return (k == 1) | (k == 7)
-
-    def detour(a, p, g):
+    def detour(i, _):
+        g = late[i]
+        a, p = g // 12, dest[g] // 2
         best = jnp.int32(-1)
         for k in (4, 3, 5, 2, 6, 1, 7):
             m = jnp.bitwise_and(p + k, 7)
             am, mp = a * 8 + m, m * 8 + p
-            last = jnp.where(route[64 + mp] < 0, 1, jnp.where((k == 1 or k == 7) & (route[128 + mp] < 0), 2, 0))
+            last = jnp.where(route[64 + mp] < 0, 1, 0)
+            if k in (1, 7):
+                last = jnp.where((last == 0) & (route[128 + mp] < 0), 2, last)
             held = route[am]
-            direct = dest[jnp.maximum(held, 0)] // 2 == m
+            direct = lax.shift_right_logical(dest[jnp.maximum(held, 0)], 1) == m
             second = jnp.where(route[64 + am] < 0, 1, jnp.where(near(a, m) & (route[128 + am] < 0), 2, 3))
             move = jnp.where(held < 0, 0, jnp.where(direct, second, 3))
             good = (last > 0) & (move < 3) & (m != a)
@@ -81,34 +81,17 @@
             am = a * 8 + m
             move = jnp.bitwise_and(best, 3)
             last = jnp.bitwise_and(best // 4, 3)
-
-            @pl.when(move > 0)
-            def _():
-                route[move * 64 + am] = route[am]
-
+            route[jnp.where(move > 0, move * 64 + am, 192)] = route[am]
             route[am] = g
             route[last * 64 + m * 8 + p] = g
 
         @pl.when(best < 0)
         def _():
-            tab[96] = 0
-
-    def spill(pair, _):
-        a, p = pair // 8, jnp.bitwise_and(pair, 7)
-        g2, g3 = route[128 + pair], route[192 + pair]
-
-        @pl.when((a != p) & (g2 >= 0) & jnp.logical_not(near(a, p)))
-        def _():
-            route[128 + pair] = -1
-            detour(a, p, g2)
-
-        @pl.when((a != p) & (g3 >= 0))
-        def _():
-            detour(a, p, g3)
-
-        return 0
-
-    lax.fori_loop(0, 64, spill, 0)
+            ok[0] = 0
+
+        return 0
+
+    lax.fori_loop(0, n_late, detour, 0)
 
     for m in range(8):
         g = route[z * 8 + m]
@@ -122,21 +105,19 @@
         from_pool = 8 + g - 12 * z
         tab[64 + j] = jnp.where(g < 0, 8, jnp.where(a == z, from_pool, a))
 
-    def final(g, source, wanted):
+    def final(g, source):
         h = jnp.maximum(g, 0)
         p = dest[h]
-
-        @pl.when(wanted & (g >= 0) & (p // 2 == z))
-        def _():
-            tab[80 + jnp.bitwise_and(p, 1) * 8 + off[h]] = source
+        mine = (g >= 0) & (lax.shift_right_logical(p, 1) == z)
+        tab[jnp.where(mine, 80 + jnp.bitwise_and(p, 1) * 8 + off[h], 115)] = source
 
     for a in range(8):
-        final(route[a * 8 + z], 8 + a, a != z)
-        final(route[64 + a * 8 + z], a, a != z)
-    final(route[128 + jnp.bitwise_and(z + 7, 7) * 8 + z], 28, True)
-    final(route[128 + jnp.bitwise_and(z + 1, 7) * 8 + z], 29, True)
+        final(route[a * 8 + z], 8 + a)
+        final(route[64 + a * 8 + z], a)
+    final(route[128 + jnp.bitwise_and(z + 7, 7) * 8 + z], 28)
+    final(route[128 + jnp.bitwise_and(z + 1, 7) * 8 + z], 29)
     for l in range(12):
-        final(12 * z + l, 16 + l, True)
+        final(12 * z + l, 16 + l)
 
 
 def padded_kernel(
@@ -430,7 +411,7 @@
     tab, master, first, second, acts, grads,
     proj_out, hidden_out, step_out,
     strip, blk, mv, gv, fv, sv,
-    send1, recv1, aold, wf, gq, gsend, grecv, gown, pk, pown, cp, q, rq,
+    send1, recv10, recv11, aold, wf, gq, gsend, grecv, gown, pk, pown, cp, qs, qr,
     hgs, hgr, hxs, hxr, hown, send5, hgf,
     ab0, pool0, xa0, fa0, sa0, sb0, xs0, xr0,
     ab1, pool1, xa1, fa1, sa1, sb1, xs1, xr1,
@@ -488,24 +469,36 @@
     for k in range(RCAP):
         blk[k] = strip[:, pl.ds(k * 128, 128)]
     for o in range(ns):
-        send1[o] = blk[tab[o]]
+        both = blk[tab[o]]
+        for h in range(2):
+            send1[h, o] = both[h * 64:(h + 1) * 64]
     locals_[1].wait()
     for b in range(BLOCKS):
         wf[d, pl.ds(b * 128, 128)] = mv[pl.ds(b * 128, 128)].astype(BF)
 
     pl.semaphore_wait(bar, ns - 1 + nt - 1 + 1)
 
-    def acopy(p, o):
-        return remote(send1.at[p], recv1.at[o], ss1.at[p], rs1.at[o], (p, t, d))
-
-    def go1(k, _):
-        acopy(sec(k), s).start()
-        return 0
-
-    lax.fori_loop(1, ns, go1, 0)
-    wcopy = remote(wf.at[d], wf.at[d], xss.at[0], xrs.at[0], dp_peer)
-    wcopy.start()
-    recv1[s] = send1[s]
+    recv1 = (recv10, recv11)
+
+    def acopy(h, p, o):
+        return remote(send1.at[h, p], recv1[h].at[o], ss1.at[h, p], rs1.at[h, o], (p, t, d))
+
+    def go1(h):
+        def go(k, _):
+            acopy(h, sec(k), s).start()
+            return 0
+
+        lax.fori_loop(1, ns, go, 0)
+
+    def weights(h):
+        rows = wf.at[d, pl.ds(h * 384, 384)]
+        return remote(rows, rows, xss.at[5 + h], xrs.at[5 + h], dp_peer)
+
+    go1(0)
+    weights(0).start()
+    go1(1)
+    for h in range(2):
+        recv1[h][s] = send1[h, s]
 
     locals_[2].wait()
     for u in range(2):
@@ -514,30 +507,35 @@
             for h in range(2):
                 gq[h, u, :, pl.ds(j * 128, 128)] = gv[:, pl.ds(h * 512 + src, 128)]
 
-    def wr1(k, _):
-        p = sec(k)
-        acopy(p, p).wait_recv()
-        return 0
-
-    lax.fori_loop(1, ns, wr1, 0)
-    for b in range(BLOCKS):
-        aold[pl.ds(trow, 128), pl.ds(b * 128, 128)] = recv1[tab[48 + b]]
-
-    def piece(i, sends, owner, device):
-        rows = aold.at[pl.ds(pl.multiple_of(owner * 128, 128), 128)]
-        return remote(rows, rows, ss2.at[sends], rs2.at[owner], device)
-
-    gx = piece(0, 0, t, x_peer)
-    gx.start()
-    for k in range(1, 4):
-        piece(0, k, t, (s, ypeer(k) * 2 + xl, d)).start()
-    piece(0, 0, tx, x_peer).wait_recv()
-    for k in range(1, 4):
-        piece(0, 3 + k, tx, (s, ypeer(k) * 2 + xl, d)).start()
+    def wr1(h):
+        def wait(k, _):
+            p = sec(k)
+            acopy(h, p, p).wait_recv()
+            return 0
+
+        lax.fori_loop(1, ns, wait, 0)
+
+    def piece(h, sends, owner, device):
+        rows = aold.at[pl.ds(pl.multiple_of(owner * 128 + h * 64, 64), 64)]
+        return remote(rows, rows, ss2.at[h, sends], rs2.at[h, owner], device)
+
+    for h in range(2):
+        wr1(h)
+        for b in range(BLOCKS):
+            aold[pl.ds(pl.multiple_of(t * 128 + h * 64, 64), 64), pl.ds(b * 128, 128)] = recv1[h][tab[48 + b]]
+        piece(h, 0, t, x_peer).start()
+        for k in range(1, 4):
+            piece(h, k, t, (s, ypeer(k) * 2 + xl, d)).start()
+    weights(1).start()
+    for h in range(2):
+        piece(h, 0, tx, x_peer).wait_recv()
+        for k in range(1, 4):
+            piece(h, 3 + k, tx, (s, ypeer(k) * 2 + xl, d)).start()
 
     nt_dims = (((1,), (1,)), ((), ()))
     tn = (((0,), (0,)), ((), ()))
-    wcopy.wait_recv()
+    for h in range(2):
+        weights(h).wait_recv()
 
     def hid(i):
         row = pl.multiple_of(i * 128, 128)
@@ -555,8 +553,9 @@
         hown[x] = hid(y * 2 + x)
 
     for k in range(1, 4):
-        piece(0, 0, ypeer(k) * 2 + xl, x_peer).wait_recv()
-        piece(0, 0, ypeer(k) * 2 + (1 - xl), x_peer).wait_recv()
+        for h in range(2):
+            piece(h, 0, ypeer(k) * 2 + xl, x_peer).wait_recv()
+            piece(h, 0, ypeer(k) * 2 + (1 - xl), x_peer).wait_recv()
 
     def grad_tile(r, h, u):
         return lax.dot_general(
@@ -595,17 +594,33 @@
 
     ccopy.wait_recv()
 
-    def qcopy(p, o):
-        return remote(q.at[p], rq.at[o], ssq.at[p], rsq.at[o], (p * 2 + c, t, d))
-
-    def go_q(k, _):
-        p = chip(k)
-        q[p] = (pown[p] + cp[p].astype(F32)).astype(BF)
-        qcopy(p, z).start()
-        return 0
-
-    lax.fori_loop(1, 8, go_q, 0)
-    rq[z] = (pown[z] + cp[z].astype(F32)).astype(BF)
+    lo, hi = pl.ds(0, 32), pl.ds(32, 32)
+
+    def ring(n, way):
+        rows = pl.ds(0, 64) if n > 1 else (lo if way == 0 else hi)
+        return remote(
+            qs.at[way, n - 1, rows], qr.at[way, n - 1, rows], ssq.at[way, n - 1], rsq.at[way, n - 1],
+            (chip(1 if way == 0 else 7) * 2 + c, t, d))
+
+    def partial_(p, rows):
+        return pown[p, rows] + cp[p, rows].astype(F32)
+
+    def ring_step(n):
+        for way in range(2):
+            p = chip(5 - n if way == 0 else n + 3)
+            first_rows, other_rows = (lo, hi) if way == 0 else (hi, lo)
+            if n > 1:
+                ring(n - 1, way).wait_recv()
+            if n == 1:
+                qs[way, 0, first_rows] = partial_(p, first_rows).astype(BF)
+            elif n == 2:
+                qs[way, 1, first_rows] = (partial_(p, first_rows) + qr[way, 0, first_rows].astype(F32)).astype(BF)
+                qs[way, 1, other_rows] = partial_(p, other_rows).astype(BF)
+            else:
+                qs[way, n - 1] = (partial_(p, pl.ds(0, 64)) + qr[way, n - 2].astype(F32)).astype(BF)
+            ring(n, way).start()
+
+    ring_step(1)
 
     parts = [
         (ab0, pool0, xa0, fa0, sa0, sb0, xs0, xr0),
@@ -711,8 +726,11 @@
     locals_[3].wait()
     locals_[4].wait()
     adam(0)
+    ring_step(2)
     round_a(0)
+    ring_step(3)
     adam(1)
+    ring_step(4)
 
     for k in range(1, 4):
         p = ypeer(k)
@@ -762,16 +780,9 @@
     hgf[pl.ds(trow, 128)] = send5[t]
     place(1)
 
-    def wr_q(k, _):
-        p = chip(k)
-        qcopy(p, p).wait_recv()
-        return 0
-
-    lax.fori_loop(1, 8, wr_q, 0)
-    acc = rq[0].astype(F32)
-    for p in range(1, 8):
-        acc = acc + rq[p].astype(F32)
-    proj_out[...] = acc.astype(BF)
+    for way in range(2):
+        ring(4, way).wait_recv()
+    proj_out[...] = (partial_(z, pl.ds(0, 64)) + qr[0, 3].astype(F32) + qr[1, 3].astype(F32)).astype(BF)
 
     def wr5(k, _):
         p = ten(k)
@@ -783,30 +794,29 @@
 
     for u in range(3):
         drain(u)
-    for cpy in (wcopy, gcopies[0], gcopies[1], ccopy, hx, gx):
+    for cpy in (gcopies[0], gcopies[1], ccopy, hx):
         cpy.wait_send()
+    for h in range(2):
+        weights(h).wait_send()
+        for i in range(7):
+            piece(h, i, t, x_peer).wait_send()
+
+        def ws(k, _):
+            acopy(h, sec(k), s).wait_send()
+            return 0
+
+        lax.fori_loop(1, ns, ws, 0)
     for k in range(1, 4):
-        piece(0, k, t, x_peer).wait_send()
-        piece(0, 3 + k, tx, x_peer).wait_send()
         hcopy(ypeer(k), y).wait_send()
-
-    def ws(k, _):
-        acopy(sec(k), s).wait_send()
-        return 0
-
-    lax.fori_loop(1, ns, ws, 0)
+    for n in range(1, 5):
+        for way in range(2):
+            ring(n, way).wait_send()
 
     def ws5(k, _):
         fcopy(ten(k), t).wait_send()
         return 0
 
     lax.fori_loop(1, nt, ws5, 0)
-
-    def ws_q(k, _):
-        qcopy(chip(k), z).wait_send()
-        return 0
-
-    lax.fori_loop(1, 8, ws_q, 0)
 
 
 def finish(proj, hidden, step, proj_out, hidden_out, step_out):
@@ -822,12 +832,12 @@
     vmem = pl.BlockSpec(memory_space=pltpu.VMEM)
     V = pltpu.VMEM
     dma = pltpu.SemaphoreType.DMA
-    tab = pl.pallas_call(
+    tab, ok = pl.pallas_call(
         plan,
-        out_shape=jax.ShapeDtypeStruct((128,), jnp.int32),
+        out_shape=(jax.ShapeDtypeStruct((128,), jnp.int32), jax.ShapeDtypeStruct((1,), jnp.int32)),
         in_specs=[smem, smem],
-        out_specs=smem,
-        scratch_shapes=[pltpu.SMEM((256,), jnp.int32)],
+        out_specs=(smem, smem),
+        scratch_shapes=[pltpu.SMEM((256,), jnp.int32), pltpu.SMEM((128,), jnp.int32)],
         name="plan",
     )(dest_section, dest_offset)
     out_shape = (
@@ -866,18 +876,18 @@
 
     routed = call(routed_kernel, [
         V((128, 1024), BF), V((8, 128, 128), BF), V((768, 512), F32), V((1024, 1024), BF), V((768, 512), F32), V((768, 512), F32),
-        V((16, 128, 128), BF), V((16, 128, 128), BF), V((1024, 768), BF), V((2, 768, 512), BF),
+        V((2, 16, 64, 128), BF), V((16, 64, 128), BF), V((16, 64, 128), BF), V((1024, 768), BF), V((2, 768, 512), BF),
         V((2, 2, 1024, 256), BF), V((2, 768, 256), BF), V((2, 768, 256), BF), V((2, 768, 256), F32),
-        V((8, 64, 1024), BF), V((8, 64, 1024), F32), V((8, 64, 1024), BF), V((8, 64, 1024), BF), V((8, 64, 1024), BF),
+        V((8, 64, 1024), BF), V((8, 64, 1024), F32), V((8, 64, 1024), BF), V((2, 4, 64, 1024), BF), V((2, 4, 64, 1024), BF),
         V((4, 2, 128, 768), BF), V((4, 2, 128, 768), BF), V((128, 768), BF), V((128, 768), BF), V((2, 128, 768), F32),
         V((8, 128, 128), BF), V((1024, 128), BF),
         *buffers(128), *buffers(128), *buffers(64),
-        dma((5,)), dma((16,)), dma((16,)), dma((8,)), dma((8,)), dma((5,)), dma((5,)), dma((8,)), dma((8,)),
+        dma((5,)), dma((2, 16)), dma((2, 16)), dma((2, 8)), dma((2, 8)), dma((7,)), dma((7,)), dma((2, 4)), dma((2, 4)),
         dma((4,)), dma((4,)), dma((8,)), dma((8,)), dma((3, 20)), dma((3, 20)),
     ], 1, "routed")
 
     args = (tab, old_master, old_first, old_second, hidden_acts[0], out_grad[0])
-    proj, hidden, step = lax.cond(tab[96] == 1, routed, padded, *args)
+    proj, hidden, step = lax.cond(ok[0] == 1, routed, padded, *args)
     proj, hidden, step = pl.pallas_call(
         finish,
         out_shape=(

time: 124 us -> 113 us (0.911)
  Pallas kernels: 122 us -> 111 us
    pallas_call x2, Pallas kernels: 120 us -> 110 us  [the longest x1 106 us: shards(): proj, hidden, step = lax.cond(ok[0] == 1, routed, padded, *args)]
where the time goes in v3:
time: 113 us
  Pallas kernels  111 us (98%)
  between operations  1.3 us (1%)
    pallas_call x1, Pallas kernels, shards(): proj, hidden, step = lax.cond(ok[0] == 1, routed, padded, *args)  106 us
    pallas_call x1, Pallas kernels, shards(): pl.pallas_call(plan, out_shape=(jax.ShapeDtypeStruct((128,), jnp.int32),...  3.4 us

profile of v3, /device:TPU:1, one launch (start us, length us, event | category | flops | bytes accessed | tf_op | source)
XLA Modules:
  0.0 112.6 jit_solution(1344170338895165204)
XLA Ops:
  0.6 3.4 %plan.1 = (s32[128]{0:T(128)S(1)}, s32[1]{0:T(128)}) custom-call(s32[96]{0:T(128)} %dest.1, s32[96]{0:T(128)} %off.1), custom_call_target="tpu_custom_call" | custom-call | tf_op jit(solution)/shard_map/plan/pallas_call | solution.py:835
  4.7 106.4 %conditional.1 = ((bf16[64,1024]{1,0:T(8,128)(2,1)S(1)}, bf16[1024,128]{1,0:T(8,128)(2,1)S(1)}, bf16[8,128,512]{2,1,0:T(8,128)(2,1)S(1)})) conditional(s32[]{:T(128)} %bitcast, (s32[128]{0:T(128)S(1)}, f32[768,512]{1,0:T(8,128)}, f32[768,512]{1,0:T(8,128)}, f32[768,512]{1,0:T(8,128)}, bf16[1024,1024]{1,0:T(8,128)(2,1)}, ...), branch_computations={%region_0.0_spmd, %region_1.0_spmd} | conditional | bytes 8 | solution.py:890
  4.9 106.2 %routed.1 = (bf16[64,1024]{1,0:T(8,128)(2,1)S(1)}, bf16[1024,128]{1,0:T(8,128)(2,1)S(1)}, bf16[8,128,512]{2,1,0:T(8,128)(2,1)S(1)}) custom-call(s32[128]{0:T(128)S(1)} %get-tuple-element.30.tab, f32[768,512]{1,0:T(8,128)} %get-tuple-element.31.master, f32[768,512]{1,0:T(8,128)} %get-tuple-element.32.first, f32[768,512]{1,0:T(8,128)} %get-tuple-element.33.second, ...), custom_call_target="tpu_custom_call" | custom-call | tf_op jit(solution)/shard_map/cond/branch_1_fun/routed/pallas_call | solution.py:890
  111.1 1.6 %finish.1 = (bf16[64,1024]{1,0:T(8,128)(2,1)}, bf16[1024,128]{1,0:T(8,128)(2,1)}, f32[1024,512]{1,0:T(8,128)}) custom-call(bf16[64,1024]{1,0:T(8,128)(2,1)S(1)} %get-tuple-element.49.proj, bf16[1024,128]{1,0:T(8,128)(2,1)S(1)} %get-tuple-element.50.hidden, bf16[8,128,512]{2,1,0:T(8,128)(2,1)S(1)} %get-tuple-element.51.step), custom_call_target="tpu_custom_call" | custom-call | tf_op jit(solution)/shard_map/finish/pallas_call | solution.py:891

commit v4 on v3

--- a/solution.py
+++ b/solution.py
@@ -519,43 +519,36 @@
         rows = aold.at[pl.ds(pl.multiple_of(owner * 128 + h * 64, 64), 64)]
         return remote(rows, rows, ss2.at[h, sends], rs2.at[h, owner], device)
 
+    up, down = ypeer(1), ypeer(3)
+
+    def at_y(q):
+        return (s, q * 2 + xl, d)
+
     for h in range(2):
         wr1(h)
         for b in range(BLOCKS):
             aold[pl.ds(pl.multiple_of(t * 128 + h * 64, 64), 64), pl.ds(b * 128, 128)] = recv1[h][tab[48 + b]]
         piece(h, 0, t, x_peer).start()
-        for k in range(1, 4):
-            piece(h, k, t, (s, ypeer(k) * 2 + xl, d)).start()
+        piece(h, 1, t, at_y(up)).start()
+        piece(h, 2, t, at_y(down)).start()
+    for h in range(2):
+        piece(h, 0, tx, x_peer).wait_recv()
+        piece(h, 3, tx, at_y(up)).start()
+        piece(h, 4, tx, at_y(down)).start()
+        piece(h, 0, up * 2 + xl, x_peer).wait_recv()
+        piece(h, 5, up * 2 + xl, at_y(down)).start()
     weights(1).start()
     for h in range(2):
-        piece(h, 0, tx, x_peer).wait_recv()
-        for k in range(1, 4):
-            piece(h, 3 + k, tx, (s, ypeer(k) * 2 + xl, d)).start()
-
+        piece(h, 0, down * 2 + (1 - xl), x_peer).wait_recv()
+        piece(h, 6, down * 2 + (1 - xl), at_y(up)).start()
     nt_dims = (((1,), (1,)), ((), ()))
     tn = (((0,), (0,)), ((), ()))
+    far = ypeer(2)
     for h in range(2):
-        weights(h).wait_recv()
-
-    def hid(i):
-        row = pl.multiple_of(i * 128, 128)
-        r = lax.dot_general(gv[pl.ds(row, 128), pl.ds(0, 512)], wf[0], nt_dims, preferred_element_type=F32)
-        return r + lax.dot_general(gv[pl.ds(row, 128), pl.ds(512, 512)], wf[1], nt_dims, preferred_element_type=F32)
-
-    def hid_y(k, _):
-        i = ypeer(k)
-        for x in range(2):
-            hgs[i, x] = hid(i * 2 + x).astype(BF)
-        return 0
-
-    lax.fori_loop(1, 4, hid_y, 0)
-    for x in range(2):
-        hown[x] = hid(y * 2 + x)
-
-    for k in range(1, 4):
-        for h in range(2):
-            piece(h, 0, ypeer(k) * 2 + xl, x_peer).wait_recv()
-            piece(h, 0, ypeer(k) * 2 + (1 - xl), x_peer).wait_recv()
+        piece(h, 0, down * 2 + xl, x_peer).wait_recv()
+        piece(h, 0, up * 2 + (1 - xl), x_peer).wait_recv()
+        piece(h, 0, far * 2 + xl, x_peer).wait_recv()
+        piece(h, 0, far * 2 + (1 - xl), x_peer).wait_recv()
 
     def grad_tile(r, h, u):
         return lax.dot_general(
@@ -568,29 +561,44 @@
         gcopies.append(remote(gsend.at[u], grecv.at[u], xss.at[1 + u], xrs.at[1 + u], dp_peer))
         gcopies[u].start()
 
-    def hcopy(i, o):
-        return remote(hgs.at[i], hgr.at[o], ssh.at[i], rsh.at[o], (s, i * 2 + xl, d))
-
-    for k in range(1, 4):
-        hcopy(ypeer(k), y).start()
+    for h in range(2):
+        weights(h).wait_recv()
 
     def proj_tile(i, _):
-        a = aold[pl.ds(pl.multiple_of(i * 128, 128), 128)]
+        a = aold[pl.ds(pl.multiple_of(i * 256, 256), 256)]
         for h in range(2):
             r = jnp.dot(a, wf[h], preferred_element_type=F32)
             cols = pl.ds(h * 512, 512)
-            lo, hi = r[:64], r[64:]
-            pk[i, :, cols] = jnp.where(c == 0, hi, lo).astype(BF)
-            pown[i, :, cols] = jnp.where(c == 0, lo, hi)
-        return 0
-
-    lax.fori_loop(0, nt, proj_tile, 0)
+            for j in range(2):
+                lo, hi = r[j * 128:j * 128 + 64], r[j * 128 + 64:j * 128 + 128]
+                pk[i * 2 + j, :, cols] = jnp.where(c == 0, hi, lo).astype(BF)
+                pown[i * 2 + j, :, cols] = jnp.where(c == 0, lo, hi)
+        return 0
+
+    lax.fori_loop(0, 4, proj_tile, 0)
     ccopy = remote(pk, cp, xss.at[3], xrs.at[3], core_peer)
     ccopy.start()
 
-    for u in range(2):
-        for r in range(3):
-            gown[u, pl.ds(r * 256, 256)] = grad_tile(r, d, u)
+    def hcopy(i, o):
+        return remote(hgs.at[i], hgr.at[o], ssh.at[i], rsh.at[o], (s, i * 2 + xl, d))
+
+    def hid(i):
+        row = pl.multiple_of(i * 256, 256)
+        r = lax.dot_general(gv[pl.ds(row, 256), pl.ds(0, 512)], wf[0], nt_dims, preferred_element_type=F32)
+        return r + lax.dot_general(gv[pl.ds(row, 256), pl.ds(512, 512)], wf[1], nt_dims, preferred_element_type=F32)
+
+    def hid_y(k, _):
+        i = ypeer(k)
+        r = hid(i).astype(BF)
+        for x in range(2):
+            hgs[i, x] = r[x * 128:(x + 1) * 128]
+        hcopy(i, y).start()
+        return 0
+
+    lax.fori_loop(1, 4, hid_y, 0)
+    r = hid(y)
+    for x in range(2):
+        hown[x] = r[x * 128:(x + 1) * 128]
 
     ccopy.wait_recv()
 
@@ -621,6 +629,9 @@
             ring(n, way).start()
 
     ring_step(1)
+    for u in range(2):
+        for r in range(3):
+            gown[u, pl.ds(r * 256, 256)] = grad_tile(r, d, u)
 
     parts = [
         (ab0, pool0, xa0, fa0, sa0, sb0, xs0, xr0),
@@ -729,8 +740,10 @@
     ring_step(2)
     round_a(0)
     ring_step(3)
+    round_b(0)
+    ring_step(4)
     adam(1)
-    ring_step(4)
+    round_a(1)
 
     for k in range(1, 4):
         p = ypeer(k)
@@ -743,9 +756,6 @@
     hxs[...] = hown[1 - xl].astype(BF)
     hx = remote(hxs, hxr, xss.at[4], xrs.at[4], x_peer)
     hx.start()
-
-    round_a(1)
-    round_b(0)
     hx.wait_recv()
     hsum = hown[xl] + hxr[...].astype(F32)
     for b in range(BLOCKS):
@@ -754,11 +764,10 @@
             ab2[j, b] = piece_[j * 64:(j + 1) * 64]
     enter(2)
     round_a(2)
+    arrive(0)
+    round_b(2)
     round_b(1)
-    round_b(2)
-    arrive(0)
     place(0)
-    arrive(1)
     arrive(2)
 
     back_copy(2).wait_recv()
@@ -778,11 +787,13 @@
 
     lax.fori_loop(1, nt, go5, 0)
     hgf[pl.ds(trow, 128)] = send5[t]
-    place(1)
+    arrive(1)
 
     for way in range(2):
         ring(4, way).wait_recv()
     proj_out[...] = (partial_(z, pl.ds(0, 64)) + qr[0, 3].astype(F32) + qr[1, 3].astype(F32)).astype(BF)
+
+    place(1)
 
     def wr5(k, _):
         p = ten(k)

time: 113 us -> 106 us (0.938)
  Pallas kernels: 111 us -> 104 us
    pallas_call x1, Pallas kernels: 106 us -> 99.1 us  [shards(): proj, hidden, step = lax.cond(ok[0] == 1, routed, padded, *args)]
where the time goes in v4:
time: 106 us
  Pallas kernels  104 us (98%)
  between operations  1.3 us (1%)
    pallas_call x1, Pallas kernels, shards(): proj, hidden, step = lax.cond(ok[0] == 1, routed, padded, *args)  99.1 us
    pallas_call x1, Pallas kernels, shards(): pl.pallas_call(plan, out_shape=(jax.ShapeDtypeStruct((128,), jnp.int32),...  3.52 us

profile of v4, /device:TPU:1, one launch (start us, length us, event | category | flops | bytes accessed | tf_op | source)
XLA Modules:
  0.0 105.7 jit_solution(8098754069285378586)
XLA Ops:
  0.6 3.5 %plan.1 = (s32[128]{0:T(128)S(1)}, s32[1]{0:T(128)}) custom-call(s32[96]{0:T(128)} %dest.1, s32[96]{0:T(128)} %off.1), custom_call_target="tpu_custom_call" | custom-call | tf_op jit(solution)/shard_map/plan/pallas_call | solution.py:846
  4.8 99.3 %conditional.1 = ((bf16[64,1024]{1,0:T(8,128)(2,1)S(1)}, bf16[1024,128]{1,0:T(8,128)(2,1)S(1)}, bf16[8,128,512]{2,1,0:T(8,128)(2,1)S(1)})) conditional(s32[]{:T(128)} %bitcast, (s32[128]{0:T(128)S(1)}, f32[768,512]{1,0:T(8,128)}, f32[768,512]{1,0:T(8,128)}, f32[768,512]{1,0:T(8,128)}, bf16[1024,1024]{1,0:T(8,128)(2,1)}, ...), branch_computations={%region_0.0_spmd, %region_1.0_spmd} | conditional | bytes 8 | solution.py:901
  5.0 99.1 %routed.1 = (bf16[64,1024]{1,0:T(8,128)(2,1)S(1)}, bf16[1024,128]{1,0:T(8,128)(2,1)S(1)}, bf16[8,128,512]{2,1,0:T(8,128)(2,1)S(1)}) custom-call(s32[128]{0:T(128)S(1)} %get-tuple-element.30.tab, f32[768,512]{1,0:T(8,128)} %get-tuple-element.31.master, f32[768,512]{1,0:T(8,128)} %get-tuple-element.32.first, f32[768,512]{1,0:T(8,128)} %get-tuple-element.33.second, ...), custom_call_target="tpu_custom_call" | custom-call | tf_op jit(solution)/shard_map/cond/branch_1_fun/routed/pallas_call | solution.py:901
  104.1 1.6 %finish.1 = (bf16[64,1024]{1,0:T(8,128)(2,1)}, bf16[1024,128]{1,0:T(8,128)(2,1)}, f32[1024,512]{1,0:T(8,128)}) custom-call(bf16[64,1024]{1,0:T(8,128)(2,1)S(1)} %get-tuple-element.49.proj, bf16[1024,128]{1,0:T(8,128)(2,1)S(1)} %get-tuple-element.50.hidden, bf16[8,128,512]{2,1,0:T(8,128)(2,1)S(1)} %get-tuple-element.51.step), custom_call_target="tpu_custom_call" | custom-call | tf_op jit(solution)/shard_map/finish/pallas_call | solution.py:902

commit v5 on v3

--- a/solution.py
+++ b/solution.py
@@ -410,8 +410,8 @@
 def routed_kernel(
     tab, master, first, second, acts, grads,
     proj_out, hidden_out, step_out,
-    strip, blk, mv, gv, fv, sv,
-    send1, recv10, recv11, aold, wf, gq, gsend, grecv, gown, pk, pown, cp, qs, qr,
+    strip, blk, mv, gv, fv, sv, av,
+    send1, recv10, recv11, aold, wf, gq, gsend, grecv, gown, gsend0, grecv0, gown0, pk, pown, cp, qs, qr,
     hgs, hgr, hxs, hxr, hown, send5, hgf,
     ab0, pool0, xa0, fa0, sa0, sb0, xs0, xr0,
     ab1, pool1, xa1, fa1, sa1, sb1, xs1, xr1,
@@ -451,9 +451,10 @@
     locals_ = [
         pltpu.make_async_copy(acts.at[pl.ds(trow, 128)], strip, lsem.at[0]),
         pltpu.make_async_copy(master, mv, lsem.at[1]),
-        pltpu.make_async_copy(grads, gv, lsem.at[2]),
         pltpu.make_async_copy(first, fv, lsem.at[3]),
         pltpu.make_async_copy(second, sv, lsem.at[4]),
+        pltpu.make_async_copy(grads, gv, lsem.at[2]),
+        pltpu.make_async_copy(acts, av, lsem.at[5]),
     ]
     for cpy in locals_:
         cpy.start()
@@ -477,150 +478,6 @@
         wf[d, pl.ds(b * 128, 128)] = mv[pl.ds(b * 128, 128)].astype(BF)
 
     pl.semaphore_wait(bar, ns - 1 + nt - 1 + 1)
-
-    recv1 = (recv10, recv11)
-
-    def acopy(h, p, o):
-        return remote(send1.at[h, p], recv1[h].at[o], ss1.at[h, p], rs1.at[h, o], (p, t, d))
-
-    def go1(h):
-        def go(k, _):
-            acopy(h, sec(k), s).start()
-            return 0
-
-        lax.fori_loop(1, ns, go, 0)
-
-    def weights(h):
-        rows = wf.at[d, pl.ds(h * 384, 384)]
-        return remote(rows, rows, xss.at[5 + h], xrs.at[5 + h], dp_peer)
-
-    go1(0)
-    weights(0).start()
-    go1(1)
-    for h in range(2):
-        recv1[h][s] = send1[h, s]
-
-    locals_[2].wait()
-    for u in range(2):
-        for j in range(2):
-            src = j * 256 + u * 128
-            for h in range(2):
-                gq[h, u, :, pl.ds(j * 128, 128)] = gv[:, pl.ds(h * 512 + src, 128)]
-
-    def wr1(h):
-        def wait(k, _):
-            p = sec(k)
-            acopy(h, p, p).wait_recv()
-            return 0
-
-        lax.fori_loop(1, ns, wait, 0)
-
-    def piece(h, sends, owner, device):
-        rows = aold.at[pl.ds(pl.multiple_of(owner * 128 + h * 64, 64), 64)]
-        return remote(rows, rows, ss2.at[h, sends], rs2.at[h, owner], device)
-
-    for h in range(2):
-        wr1(h)
-        for b in range(BLOCKS):
-            aold[pl.ds(pl.multiple_of(t * 128 + h * 64, 64), 64), pl.ds(b * 128, 128)] = recv1[h][tab[48 + b]]
-        piece(h, 0, t, x_peer).start()
-        for k in range(1, 4):
-            piece(h, k, t, (s, ypeer(k) * 2 + xl, d)).start()
-    weights(1).start()
-    for h in range(2):
-        piece(h, 0, tx, x_peer).wait_recv()
-        for k in range(1, 4):
-            piece(h, 3 + k, tx, (s, ypeer(k) * 2 + xl, d)).start()
-
-    nt_dims = (((1,), (1,)), ((), ()))
-    tn = (((0,), (0,)), ((), ()))
-    for h in range(2):
-        weights(h).wait_recv()
-
-    def hid(i):
-        row = pl.multiple_of(i * 128, 128)
-        r = lax.dot_general(gv[pl.ds(row, 128), pl.ds(0, 512)], wf[0], nt_dims, preferred_element_type=F32)
-        return r + lax.dot_general(gv[pl.ds(row, 128), pl.ds(512, 512)], wf[1], nt_dims, preferred_element_type=F32)
-
-    def hid_y(k, _):
-        i = ypeer(k)
-        for x in range(2):
-            hgs[i, x] = hid(i * 2 + x).astype(BF)
-        return 0
-
-    lax.fori_loop(1, 4, hid_y, 0)
-    for x in range(2):
-        hown[x] = hid(y * 2 + x)
-
-    for k in range(1, 4):
-        for h in range(2):
-            piece(h, 0, ypeer(k) * 2 + xl, x_peer).wait_recv()
-            piece(h, 0, ypeer(k) * 2 + (1 - xl), x_peer).wait_recv()
-
-    def grad_tile(r, h, u):
-        return lax.dot_general(
-            aold[:, pl.ds(r * 256, 256)], gq[h, u], tn, preferred_element_type=F32) * (1.0 / 2048.0)
-
-    gcopies = []
-    for u in range(2):
-        for r in range(3):
-            gsend[u, pl.ds(r * 256, 256)] = grad_tile(r, od, u).astype(BF)
-        gcopies.append(remote(gsend.at[u], grecv.at[u], xss.at[1 + u], xrs.at[1 + u], dp_peer))
-        gcopies[u].start()
-
-    def hcopy(i, o):
-        return remote(hgs.at[i], hgr.at[o], ssh.at[i], rsh.at[o], (s, i * 2 + xl, d))
-
-    for k in range(1, 4):
-        hcopy(ypeer(k), y).start()
-
-    def proj_tile(i, _):
-        a = aold[pl.ds(pl.multiple_of(i * 128, 128), 128)]
-        for h in range(2):
-            r = jnp.dot(a, wf[h], preferred_element_type=F32)
-            cols = pl.ds(h * 512, 512)
-            lo, hi = r[:64], r[64:]
-            pk[i, :, cols] = jnp.where(c == 0, hi, lo).astype(BF)
-            pown[i, :, cols] = jnp.where(c == 0, lo, hi)
-        return 0
-
-    lax.fori_loop(0, nt, proj_tile, 0)
-    ccopy = remote(pk, cp, xss.at[3], xrs.at[3], core_peer)
-    ccopy.start()
-
-    for u in range(2):
-        for r in range(3):
-            gown[u, pl.ds(r * 256, 256)] = grad_tile(r, d, u)
-
-    ccopy.wait_recv()
-
-    lo, hi = pl.ds(0, 32), pl.ds(32, 32)
-
-    def ring(n, way):
-        rows = pl.ds(0, 64) if n > 1 else (lo if way == 0 else hi)
-        return remote(
-            qs.at[way, n - 1, rows], qr.at[way, n - 1, rows], ssq.at[way, n - 1], rsq.at[way, n - 1],
-            (chip(1 if way == 0 else 7) * 2 + c, t, d))
-
-    def partial_(p, rows):
-        return pown[p, rows] + cp[p, rows].astype(F32)
-
-    def ring_step(n):
-        for way in range(2):
-            p = chip(5 - n if way == 0 else n + 3)
-            first_rows, other_rows = (lo, hi) if way == 0 else (hi, lo)
-            if n > 1:
-                ring(n - 1, way).wait_recv()
-            if n == 1:
-                qs[way, 0, first_rows] = partial_(p, first_rows).astype(BF)
-            elif n == 2:
-                qs[way, 1, first_rows] = (partial_(p, first_rows) + qr[way, 0, first_rows].astype(F32)).astype(BF)
-                qs[way, 1, other_rows] = partial_(p, other_rows).astype(BF)
-            else:
-                qs[way, n - 1] = (partial_(p, pl.ds(0, 64)) + qr[way, n - 2].astype(F32)).astype(BF)
-            ring(n, way).start()
-
-    ring_step(1)
 
     parts = [
         (ab0, pool0, xa0, fa0, sa0, sb0, xs0, xr0),
@@ -701,18 +558,207 @@
         for j in range(2):
             copy_n(u, j).wait_send()
 
-    def adam(u):
-        gcopies[u].wait_recv()
+    def step_of(f0, s0, own, other):
+        g = own + other.astype(F32)
+        f1 = 0.9 * f0 + 0.1 * g
+        s1 = 0.999 * s0 + 0.001 * g * g
+        return (f1 / (jnp.sqrt(s1 / CORR_SECOND) + 1e-08)).astype(BF)
+
+    recv1 = (recv10, recv11)
+
+    def acopy(h, p, o):
+        return remote(send1.at[h, p], recv1[h].at[o], ss1.at[h, p], rs1.at[h, o], (p, t, d))
+
+    def go1(h):
+        def go(k, _):
+            acopy(h, sec(k), s).start()
+            return 0
+
+        lax.fori_loop(1, ns, go, 0)
+
+    def weights(h):
+        rows = wf.at[d, pl.ds(h * 384, 384)]
+        return remote(rows, rows, xss.at[5 + h], xrs.at[5 + h], dp_peer)
+
+    go1(0)
+    weights(0).start()
+    go1(1)
+    for h in range(2):
+        recv1[h][s] = send1[h, s]
+
+    locals_[2].wait()
+    locals_[3].wait()
+    for b in range(BLOCKS):
+        rows = pl.ds(b * 128, 128)
+        for j in range(2):
+            ab0[j, b, pl.ds(0, 128)] = fv[rows, pl.ds(j * 256, 128)].astype(BF)
+            ab0[j, b, pl.ds(128, 128)] = sv[rows, pl.ds(j * 256, 128)].astype(BF)
+    enter(0)
+
+    locals_[4].wait()
+    for u in range(2):
+        for j in range(2):
+            src = j * 256 + u * 128
+            for h in range(2):
+                gq[h, u, :, pl.ds(j * 128, 128)] = gv[:, pl.ds(h * 512 + src, 128)]
+
+    nt_dims = (((1,), (1,)), ((), ()))
+    tn = (((0,), (0,)), ((), ()))
+    locals_[5].wait()
+
+    def grad_here(r, h):
+        return lax.dot_general(
+            av[:, pl.ds(r * 256, 256)], gq[h, 0], tn, preferred_element_type=F32) * (1.0 / 2048.0)
+
+    for r in range(4):
+        gsend0[pl.ds(r * 256, 256)] = grad_here(r, od).astype(BF)
+        gown0[pl.ds(r * 256, 256)] = grad_here(r, d)
+    gcopy0 = remote(gsend0, grecv0, xss.at[1], xrs.at[1], dp_peer)
+
+    def wr1(h):
+        def wait(k, _):
+            p = sec(k)
+            acopy(h, p, p).wait_recv()
+            return 0
+
+        lax.fori_loop(1, ns, wait, 0)
+
+    def piece(h, sends, owner, device):
+        rows = aold.at[pl.ds(pl.multiple_of(owner * 128 + h * 64, 64), 64)]
+        return remote(rows, rows, ss2.at[h, sends], rs2.at[h, owner], device)
+
+    up, down = ypeer(1), ypeer(3)
+
+    def at_y(q):
+        return (s, q * 2 + xl, d)
+
+    for h in range(2):
+        wr1(h)
+        for b in range(BLOCKS):
+            aold[pl.ds(pl.multiple_of(t * 128 + h * 64, 64), 64), pl.ds(b * 128, 128)] = recv1[h][tab[48 + b]]
+        piece(h, 0, t, x_peer).start()
+        piece(h, 1, t, at_y(up)).start()
+        piece(h, 2, t, at_y(down)).start()
+        if h == 1:
+            round_a(0)
+        piece(h, 0, tx, x_peer).wait_recv()
+        piece(h, 3, tx, at_y(up)).start()
+        piece(h, 4, tx, at_y(down)).start()
+        if h == 0:
+            weights(1).start()
+        piece(h, 0, up * 2 + xl, x_peer).wait_recv()
+        piece(h, 5, up * 2 + xl, at_y(down)).start()
+        piece(h, 0, down * 2 + (1 - xl), x_peer).wait_recv()
+        piece(h, 6, down * 2 + (1 - xl), at_y(up)).start()
+
+    for h in range(2):
+        weights(h).wait_recv()
+
+    def hcopy(i, o):
+        return remote(hgs.at[i], hgr.at[o], ssh.at[i], rsh.at[o], (s, i * 2 + xl, d))
+
+    def hid(i):
+        row = pl.multiple_of(i * 256, 256)
+        r = lax.dot_general(gv[pl.ds(row, 256), pl.ds(0, 512)], wf[0], nt_dims, preferred_element_type=F32)
+        return r + lax.dot_general(gv[pl.ds(row, 256), pl.ds(512, 512)], wf[1], nt_dims, preferred_element_type=F32)
+
+    def hid_y(k, _):
+        i = ypeer(k)
+        r = hid(i).astype(BF)
+        for x in range(2):
+            hgs[i, x] = r[x * 128:(x + 1) * 128]
+        hcopy(i, y).start()
+        return 0
+
+    lax.fori_loop(1, 4, hid_y, 0)
+    r = hid(y)
+    for x in range(2):
+        hown[x] = r[x * 128:(x + 1) * 128]
+    far = ypeer(2)
+    for h in range(2):
+        piece(h, 0, down * 2 + xl, x_peer).wait_recv()
+        piece(h, 0, up * 2 + (1 - xl), x_peer).wait_recv()
+        piece(h, 0, far * 2 + xl, x_peer).wait_recv()
+        piece(h, 0, far * 2 + (1 - xl), x_peer).wait_recv()
+
+    def grad_tile(r, h):
+        return lax.dot_general(
+            aold[:, pl.ds(r * 256, 256)], gq[h, 1], tn, preferred_element_type=F32) * (1.0 / 2048.0)
+
+    for r in range(3):
+        gsend[pl.ds(r * 256, 256)] = grad_tile(r, od).astype(BF)
+    gcopy = remote(gsend, grecv, xss.at[2], xrs.at[2], dp_peer)
+    gcopy.start()
+    round_b(0)
+
+    def proj_tile(i, _):
+        a = aold[pl.ds(pl.multiple_of(i * 256, 256), 256)]
+        for h in range(2):
+            r = jnp.dot(a, wf[h], preferred_element_type=F32)
+            cols = pl.ds(h * 512, 512)
+            for j in range(2):
+                lo, hi = r[j * 128:j * 128 + 64], r[j * 128 + 64:j * 128 + 128]
+                pk[i * 2 + j, :, cols] = jnp.where(c == 0, hi, lo).astype(BF)
+                pown[i * 2 + j, :, cols] = jnp.where(c == 0, lo, hi)
+        return 0
+
+    lax.fori_loop(0, 4, proj_tile, 0)
+    ccopy = remote(pk, cp, xss.at[3], xrs.at[3], core_peer)
+    ccopy.start()
+
+    for r in range(3):
+        gown[pl.ds(r * 256, 256)] = grad_tile(r, d)
+
+    ccopy.wait_recv()
+
+    lo, hi = pl.ds(0, 32), pl.ds(32, 32)
+
+    def ring(n, way):
+        rows = pl.ds(0, 64) if n > 1 else (lo if way == 0 else hi)
+        return remote(
+            qs.at[way, n - 1, rows], qr.at[way, n - 1, rows], ssq.at[way, n - 1], rsq.at[way, n - 1],
+            (chip(1 if way == 0 else 7) * 2 + c, t, d))
+
+    def partial_(p, rows):
+        return pown[p, rows] + cp[p, rows].astype(F32)
+
+    def ring_step(n):
+        for way in range(2):
+            p = chip(5 - n if way == 0 else n + 3)
+            first_rows, other_rows = (lo, hi) if way == 0 else (hi, lo)
+            if n > 1:
+                ring(n - 1, way).wait_recv()
+            if n == 1:
+                qs[way, 0, first_rows] = partial_(p, first_rows).astype(BF)
+            elif n == 2:
+                qs[way, 1, first_rows] = (partial_(p, first_rows) + qr[way, 0, first_rows].astype(F32)).astype(BF)
+                qs[way, 1, other_rows] = partial_(p, other_rows).astype(BF)
+            else:
+                qs[way, n - 1] = (partial_(p, pl.ds(0, 64)) + qr[way, n - 2].astype(F32)).astype(BF)
+            ring(n, way).start()
+
+    def adam():
+        gcopy.wait_recv()
         for b in range(BLOCKS):
             rows = pl.ds(b * 128, 128)
             for j in range(2):
-                cols = pl.ds(j * 256 + u * 128, 128)
+                cols = pl.ds(j * 256 + 128, 128)
                 here = pl.ds(j * 128, 128)
-                g = gown[u, rows, here] + grecv[u, rows, here].astype(F32)
-                f1 = 0.9 * fv[rows, cols] + 0.1 * g
-                s1 = 0.999 * sv[rows, cols] + 0.001 * g * g
-                parts[u][0][j, b] = (f1 / (jnp.sqrt(s1 / CORR_SECOND) + 1e-08)).astype(BF)
-        enter(u)
+                ab1[j, b] = step_of(fv[rows, cols], sv[rows, cols], gown[rows, here], grecv[rows, here])
+        enter(1)
+
+    def place_mine():
+        back_copy(0).wait_recv()
+        gcopy0.wait_recv()
+        for k in range(RCAP):
+            used = tab[40 + k].astype(F32)
+            rows = pl.ds(k * 128, 128)
+            for j in range(2):
+                both = fa0[tab[80 + c * 8 + k]] if j == 0 else xr0[k]
+                half = c if j == 0 else oc
+                here = pl.ds(pl.multiple_of(half * 128, 128), 128)
+                st = step_of(both[:128].astype(F32), both[128:].astype(F32), gown0[rows, here], grecv0[rows, here])
+                step_out[k, :, pl.ds(pl.multiple_of(half * 256, 128), 128)] = (st.astype(F32) * used).astype(BF)
 
     def place(u):
         fa_, xr_ = parts[u][3], parts[u][7]
@@ -723,14 +769,12 @@
             step_out[k, :, mine] = fa_[tab[80 + c * 8 + k]]
             step_out[k, :, theirs] = xr_[k]
 
-    locals_[3].wait()
-    locals_[4].wait()
-    adam(0)
+    ring_step(1)
+    adam()
+    gcopy0.start()
     ring_step(2)
-    round_a(0)
+    round_a(1)
     ring_step(3)
-    adam(1)
-    ring_step(4)
 
     for k in range(1, 4):
         p = ypeer(k)
@@ -743,9 +787,7 @@
     hxs[...] = hown[1 - xl].astype(BF)
     hx = remote(hxs, hxr, xss.at[4], xrs.at[4], x_peer)
     hx.start()
-
-    round_a(1)
-    round_b(0)
+    ring_step(4)
     hx.wait_recv()
     hsum = hown[xl] + hxr[...].astype(F32)
     for b in range(BLOCKS):
@@ -754,11 +796,10 @@
             ab2[j, b] = piece_[j * 64:(j + 1) * 64]
     enter(2)
     round_a(2)
+    arrive(0)
+    round_b(2)
     round_b(1)
-    round_b(2)
-    arrive(0)
-    place(0)
-    arrive(1)
+    place_mine()
     arrive(2)
 
     back_copy(2).wait_recv()
@@ -778,12 +819,14 @@
 
     lax.fori_loop(1, nt, go5, 0)
     hgf[pl.ds(trow, 128)] = send5[t]
-    place(1)
+    arrive(1)
 
     for way in range(2):
         ring(4, way).wait_recv()
     proj_out[...] = (partial_(z, pl.ds(0, 64)) + qr[0, 3].astype(F32) + qr[1, 3].astype(F32)).astype(BF)
 
+    place(1)
+
     def wr5(k, _):
         p = ten(k)
         fcopy(p, p).wait_recv()
@@ -794,7 +837,7 @@
 
     for u in range(3):
         drain(u)
-    for cpy in (gcopies[0], gcopies[1], ccopy, hx):
+    for cpy in (gcopy0, gcopy, ccopy, hx):
         cpy.wait_send()
     for h in range(2):
         weights(h).wait_send()
@@ -875,14 +918,15 @@
         return [V((*n, rows, 128), BF) for n in shapes]
 
     routed = call(routed_kernel, [
-        V((128, 1024), BF), V((8, 128, 128), BF), V((768, 512), F32), V((1024, 1024), BF), V((768, 512), F32), V((768, 512), F32),
+        V((128, 1024), BF), V((8, 128, 128), BF), V((768, 512), F32), V((1024, 1024), BF), V((768, 512), F32), V((768, 512), F32), V((1024, 1024), BF),
         V((2, 16, 64, 128), BF), V((16, 64, 128), BF), V((16, 64, 128), BF), V((1024, 768), BF), V((2, 768, 512), BF),
-        V((2, 2, 1024, 256), BF), V((2, 768, 256), BF), V((2, 768, 256), BF), V((2, 768, 256), F32),
+        V((2, 2, 1024, 256), BF), V((768, 256), BF), V((768, 256), BF), V((768, 256), F32),
+        V((1024, 256), BF), V((1024, 256), BF), V((1024, 256), F32),
         V((8, 64, 1024), BF), V((8, 64, 1024), F32), V((8, 64, 1024), BF), V((2, 4, 64, 1024), BF), V((2, 4, 64, 1024), BF),
         V((4, 2, 128, 768), BF), V((4, 2, 128, 768), BF), V((128, 768), BF), V((128, 768), BF), V((2, 128, 768), F32),
         V((8, 128, 128), BF), V((1024, 128), BF),
-        *buffers(128), *buffers(128), *buffers(64),
-        dma((5,)), dma((2, 16)), dma((2, 16)), dma((2, 8)), dma((2, 8)), dma((7,)), dma((7,)), dma((2, 4)), dma((2, 4)),
+        *buffers(256), *buffers(128), *buffers(64),
+        dma((6,)), dma((2, 16)), dma((2, 16)), dma((2, 8)), dma((2, 8)), dma((7,)), dma((7,)), dma((2, 4)), dma((2, 4)),
         dma((4,)), dma((4,)), dma((8,)), dma((8,)), dma((3, 20)), dma((3, 20)),
     ], 1, "routed")
 

time: 113 us -> 103 us (0.912)
  Pallas kernels: 111 us -> 102 us
    pallas_call x1, Pallas kernels: 106 us -> 96.4 us  [shards(): proj, hidden, step = lax.cond(ok[0] == 1, routed, padded, *args)]
where the time goes in v5:
time: 103 us
  Pallas kernels  102 us (99%)
  between operations  1.3 us (1%)
    pallas_call x1, Pallas kernels, shards(): proj, hidden, step = lax.cond(ok[0] == 1, routed, padded, *args)  96.4 us
    pallas_call x1, Pallas kernels, shards(): pl.pallas_call(plan, out_shape=(jax.ShapeDtypeStruct((128,), jnp.int32),...  3.52 us

profile of v5, /device:TPU:1, one launch (start us, length us, event | category | flops | bytes accessed | tf_op | source)
XLA Modules:
  0.0 103.0 jit_solution(8921619904599329240)
XLA Ops:
  0.6 3.5 %plan.1 = (s32[128]{0:T(128)S(1)}, s32[1]{0:T(128)}) custom-call(s32[96]{0:T(128)} %dest.1, s32[96]{0:T(128)} %off.1), custom_call_target="tpu_custom_call" | custom-call | tf_op jit(solution)/shard_map/plan/pallas_call | solution.py:878
  4.8 96.6 %conditional.1 = ((bf16[64,1024]{1,0:T(8,128)(2,1)S(1)}, bf16[1024,128]{1,0:T(8,128)(2,1)S(1)}, bf16[8,128,512]{2,1,0:T(8,128)(2,1)S(1)})) conditional(s32[]{:T(128)} %bitcast, (s32[128]{0:T(128)S(1)}, f32[768,512]{1,0:T(8,128)}, f32[768,512]{1,0:T(8,128)}, f32[768,512]{1,0:T(8,128)}, bf16[1024,1024]{1,0:T(8,128)(2,1)}, ...), branch_computations={%region_0.0_spmd, %region_1.0_spmd} | conditional | bytes 8 | solution.py:934
  5.0 96.4 %routed.1 = (bf16[64,1024]{1,0:T(8,128)(2,1)S(1)}, bf16[1024,128]{1,0:T(8,128)(2,1)S(1)}, bf16[8,128,512]{2,1,0:T(8,128)(2,1)S(1)}) custom-call(s32[128]{0:T(128)S(1)} %get-tuple-element.30.tab, f32[768,512]{1,0:T(8,128)} %get-tuple-element.31.master, f32[768,512]{1,0:T(8,128)} %get-tuple-element.32.first, f32[768,512]{1,0:T(8,128)} %get-tuple-element.33.second, ...), custom_call_target="tpu_custom_call" | custom-call | tf_op jit(solution)/shard_map/cond/branch_1_fun/routed/pallas_call | solution.py:934
  101.4 1.6 %finish.1 = (bf16[64,1024]{1,0:T(8,128)(2,1)}, bf16[1024,128]{1,0:T(8,128)(2,1)}, f32[1024,512]{1,0:T(8,128)}) custom-call(bf16[64,1024]{1,0:T(8,128)(2,1)S(1)} %get-tuple-element.49.proj, bf16[1024,128]{1,0:T(8,128)(2,1)S(1)} %get-tuple-element.50.hidden, bf16[8,128,512]{2,1,0:T(8,128)(2,1)S(1)} %get-tuple-element.51.step), custom_call_target="tpu_custom_call" | custom-call | tf_op jit(solution)/shard_map/finish/pallas_call | solution.py:935

commit v6 on v5

--- a/solution.py
+++ b/solution.py
@@ -570,11 +570,10 @@
         return remote(send1.at[h, p], recv1[h].at[o], ss1.at[h, p], rs1.at[h, o], (p, t, d))
 
     def go1(h):
-        def go(k, _):
-            acopy(h, sec(k), s).start()
-            return 0
-
-        lax.fori_loop(1, ns, go, 0)
+        for k in (4, 3, 5, 2, 6, 1, 7):
+            for e in (c, oc):
+                acopy(h, chip(k) * 2 + e, s).start()
+        acopy(h, z * 2 + oc, s).start()
 
     def weights(h):
         rows = wf.at[d, pl.ds(h * 384, 384)]
@@ -639,41 +638,18 @@
         piece(h, 0, t, x_peer).start()
         piece(h, 1, t, at_y(up)).start()
         piece(h, 2, t, at_y(down)).start()
-        if h == 1:
-            round_a(0)
+    round_a(0)
+    for h in range(2):
         piece(h, 0, tx, x_peer).wait_recv()
         piece(h, 3, tx, at_y(up)).start()
         piece(h, 4, tx, at_y(down)).start()
-        if h == 0:
-            weights(1).start()
         piece(h, 0, up * 2 + xl, x_peer).wait_recv()
         piece(h, 5, up * 2 + xl, at_y(down)).start()
+    weights(1).start()
+    for h in range(2):
         piece(h, 0, down * 2 + (1 - xl), x_peer).wait_recv()
         piece(h, 6, down * 2 + (1 - xl), at_y(up)).start()
 
-    for h in range(2):
-        weights(h).wait_recv()
-
-    def hcopy(i, o):
-        return remote(hgs.at[i], hgr.at[o], ssh.at[i], rsh.at[o], (s, i * 2 + xl, d))
-
-    def hid(i):
-        row = pl.multiple_of(i * 256, 256)
-        r = lax.dot_general(gv[pl.ds(row, 256), pl.ds(0, 512)], wf[0], nt_dims, preferred_element_type=F32)
-        return r + lax.dot_general(gv[pl.ds(row, 256), pl.ds(512, 512)], wf[1], nt_dims, preferred_element_type=F32)
-
-    def hid_y(k, _):
-        i = ypeer(k)
-        r = hid(i).astype(BF)
-        for x in range(2):
-            hgs[i, x] = r[x * 128:(x + 1) * 128]
-        hcopy(i, y).start()
-        return 0
-
-    lax.fori_loop(1, 4, hid_y, 0)
-    r = hid(y)
-    for x in range(2):
-        hown[x] = r[x * 128:(x + 1) * 128]
     far = ypeer(2)
     for h in range(2):
         piece(h, 0, down * 2 + xl, x_peer).wait_recv()
@@ -690,6 +666,9 @@
     gcopy = remote(gsend, grecv, xss.at[2], xrs.at[2], dp_peer)
     gcopy.start()
     round_b(0)
+
+    for h in range(2):
+        weights(h).wait_recv()
 
     def proj_tile(i, _):
         a = aold[pl.ds(pl.multiple_of(i * 256, 256), 256)]
@@ -705,6 +684,28 @@
     lax.fori_loop(0, 4, proj_tile, 0)
     ccopy = remote(pk, cp, xss.at[3], xrs.at[3], core_peer)
     ccopy.start()
+
+    def hcopy(i, o):
+        return remote(hgs.at[i], hgr.at[o], ssh.at[i], rsh.at[o], (s, i * 2 + xl, d))
+
+    def hid(i):
+        row = pl.multiple_of(i * 256, 256)
+        r = lax.dot_general(gv[pl.ds(row, 256), pl.ds(0, 512)], wf[0], nt_dims, preferred_element_type=F32)
+        return r + lax.dot_general(gv[pl.ds(row, 256), pl.ds(512, 512)], wf[1], nt_dims, preferred_element_type=F32)
+
+    def hid_y(k, _):
+        i = ypeer(k)
+        r = hid(i).astype(BF)
+        for x in range(2):
+            hgs[i, x] = r[x * 128:(x + 1) * 128]
+        hcopy(i, y).start()
+        return 0
+
+    lax.fori_loop(1, 4, hid_y, 0)
+    r = hid(y)
+    for x in range(2):
+        hown[x] = r[x * 128:(x + 1) * 128]
+
 
     for r in range(3):
         gown[pl.ds(r * 256, 256)] = grad_tile(r, d)

time: 103 us -> 98 us (0.951)
  Pallas kernels: 102 us -> 96.4 us
    pallas_call x1, Pallas kernels: 96.4 us -> 91.5 us  [shards(): proj, hidden, step = lax.cond(ok[0] == 1, routed, padded, *args)]
where the time goes in v6:
time: 98 us; the launch traced here: 97.9 us
  Pallas kernels  96.4 us (98%)
  between operations  1.3 us (1%)
    pallas_call x1, Pallas kernels, shards(): proj, hidden, step = lax.cond(ok[0] == 1, routed, padded, *args)  91.5 us
    pallas_call x1, Pallas kernels, shards(): pl.pallas_call(plan, out_shape=(jax.ShapeDtypeStruct((128,), jnp.int32),...  3.28 us

profile of v6, /device:TPU:1, one launch (start us, length us, event | category | flops | bytes accessed | tf_op | source)
XLA Modules:
  0.0 97.9 jit_solution(10358075607539659862)
XLA Ops:
  0.6 3.3 %plan.1 = (s32[128]{0:T(128)S(1)}, s32[1]{0:T(128)}) custom-call(s32[96]{0:T(128)} %dest.1, s32[96]{0:T(128)} %off.1), custom_call_target="tpu_custom_call" | custom-call | tf_op jit(solution)/shard_map/plan/pallas_call | solution.py:879
  4.6 91.7 %conditional.1 = ((bf16[64,1024]{1,0:T(8,128)(2,1)S(1)}, bf16[1024,128]{1,0:T(8,128)(2,1)S(1)}, bf16[8,128,512]{2,1,0:T(8,128)(2,1)S(1)})) conditional(s32[]{:T(128)} %bitcast, (s32[128]{0:T(128)S(1)}, f32[768,512]{1,0:T(8,128)}, f32[768,512]{1,0:T(8,128)}, f32[768,512]{1,0:T(8,128)}, bf16[1024,1024]{1,0:T(8,128)(2,1)}, ...), branch_computations={%region_0.0_spmd, %region_1.0_spmd} | conditional | bytes 8 | solution.py:935
  4.8 91.5 %routed.1 = (bf16[64,1024]{1,0:T(8,128)(2,1)S(1)}, bf16[1024,128]{1,0:T(8,128)(2,1)S(1)}, bf16[8,128,512]{2,1,0:T(8,128)(2,1)S(1)}) custom-call(s32[128]{0:T(128)S(1)} %get-tuple-element.30.tab, f32[768,512]{1,0:T(8,128)} %get-tuple-element.31.master, f32[768,512]{1,0:T(8,128)} %get-tuple-element.32.first, f32[768,512]{1,0:T(8,128)} %get-tuple-element.33.second, ...), custom_call_target="tpu_custom_call" | custom-call | tf_op jit(solution)/shard_map/cond/branch_1_fun/routed/pallas_call | solution.py:935
  96.3 1.6 %finish.1 = (bf16[64,1024]{1,0:T(8,128)(2,1)}, bf16[1024,128]{1,0:T(8,128)(2,1)}, f32[1024,512]{1,0:T(8,128)}) custom-call(bf16[64,1024]{1,0:T(8,128)(2,1)S(1)} %get-tuple-element.49.proj, bf16[1024,128]{1,0:T(8,128)(2,1)S(1)} %get-tuple-element.50.hidden, bf16[8,128,512]{2,1,0:T(8,128)(2,1)S(1)} %get-tuple-element.51.step), custom_call_target="tpu_custom_call" | custom-call | tf_op jit(solution)/shard_map/finish/pallas_call | solution.py:936

commit v7 on v6

--- a/solution.py
+++ b/solution.py
@@ -797,10 +797,9 @@
             ab2[j, b] = piece_[j * 64:(j + 1) * 64]
     enter(2)
     round_a(2)
-    arrive(0)
     round_b(2)
     round_b(1)
-    place_mine()
+    arrive(0)
     arrive(2)
 
     back_copy(2).wait_recv()
@@ -820,6 +819,7 @@
 
     lax.fori_loop(1, nt, go5, 0)
     hgf[pl.ds(trow, 128)] = send5[t]
+    place_mine()
     arrive(1)
 
     for way in range(2):

time: 98 us -> 98.1 us (level)
  no operation moved by 1% of the time
where the time goes in v7:
time: 98.1 us; the launch traced here: 98 us
  Pallas kernels  96.5 us (98%)
  between operations  1.3 us (1%)
    pallas_call x1, Pallas kernels, shards(): proj, hidden, step = lax.cond(ok[0] == 1, routed, padded, *args)  91.6 us
    pallas_call x1, Pallas kernels, shards(): pl.pallas_call(plan, out_shape=(jax.ShapeDtypeStruct((128,), jnp.int32),...  3.4 us

profile of v7, /device:TPU:1, one launch (start us, length us, event | category | flops | bytes accessed | tf_op | source)
XLA Modules:
  0.0 98.0 jit_solution(8984043967717734525)
XLA Ops:
  0.6 3.4 %plan.1 = (s32[128]{0:T(128)S(1)}, s32[1]{0:T(128)}) custom-call(s32[96]{0:T(128)} %dest.1, s32[96]{0:T(128)} %off.1), custom_call_target="tpu_custom_call" | custom-call | tf_op jit(solution)/shard_map/plan/pallas_call | solution.py:879
  4.7 91.8 %conditional.1 = ((bf16[64,1024]{1,0:T(8,128)(2,1)S(1)}, bf16[1024,128]{1,0:T(8,128)(2,1)S(1)}, bf16[8,128,512]{2,1,0:T(8,128)(2,1)S(1)})) conditional(s32[]{:T(128)} %bitcast, (s32[128]{0:T(128)S(1)}, f32[768,512]{1,0:T(8,128)}, f32[768,512]{1,0:T(8,128)}, f32[768,512]{1,0:T(8,128)}, bf16[1024,1024]{1,0:T(8,128)(2,1)}, ...), branch_computations={%region_0.0_spmd, %region_1.0_spmd} | conditional | bytes 8 | solution.py:935
  4.9 91.6 %routed.1 = (bf16[64,1024]{1,0:T(8,128)(2,1)S(1)}, bf16[1024,128]{1,0:T(8,128)(2,1)S(1)}, bf16[8,128,512]{2,1,0:T(8,128)(2,1)S(1)}) custom-call(s32[128]{0:T(128)S(1)} %get-tuple-element.30.tab, f32[768,512]{1,0:T(8,128)} %get-tuple-element.31.master, f32[768,512]{1,0:T(8,128)} %get-tuple-element.32.first, f32[768,512]{1,0:T(8,128)} %get-tuple-element.33.second, ...), custom_call_target="tpu_custom_call" | custom-call | tf_op jit(solution)/shard_map/cond/branch_1_fun/routed/pallas_call | solution.py:935
  96.5 1.6 %finish.1 = (bf16[64,1024]{1,0:T(8,128)(2,1)}, bf16[1024,128]{1,0:T(8,128)(2,1)}, f32[1024,512]{1,0:T(8,128)}) custom-call(bf16[64,1024]{1,0:T(8,128)(2,1)S(1)} %get-tuple-element.49.proj, bf16[1024,128]{1,0:T(8,128)(2,1)S(1)} %get-tuple-element.50.hidden, bf16[8,128,512]{2,1,0:T(8,128)(2,1)S(1)} %get-tuple-element.51.step), custom_call_target="tpu_custom_call" | custom-call | tf_op jit(solution)/shard_map/finish/pallas_call | solution.py:936
